TPU v7x, 128 devices: a whole 4x4x4 slice. The times are simulated.
128 devices in a mesh: rows: 32 (over x, y, core), rep: 4 (over z).
Axes of the slice: x: 4, y: 4, z: 4, core: 2. Of those that a mesh axis runs over, the one named last changes fastest.
Arguments:
- vectors: bfloat16 [65536, 1024], P(('rows', 'rep')), may hold values from -96 to 96
- list_ids: int32 [65536], P(('rows', 'rep')), may hold values from 0 to 262143, as said below
- centroids: bfloat16 [262144, 1024], P(('rows', 'rep')), may hold values from -16 to 16
- list_place: int32 [262144], replicated, may hold values from 0 to 262143, as said below
- codes_first: int32 [65536, 128], P(('rows', 'rep')), may hold values from 0 to 255
- codes_second: int32 [65536, 128], P(('rows', 'rep')), may hold values from 0 to 255
Outputs:
- codebook_first: float32 [256, 1024], P(None, 'rows')
- codebook_second: float32 [256, 1024], P(None, 'rows')
Inputs may be any that keep to these rules, and one draw needn't show every extreme that they name: list_place is a permutation of the table rows. Among the rows of one device, at most 8 have list_place[list_ids] inside one device's block of 2048 table rows, and exactly 8 for some blocks of every device.
All inputs are finite; a program needn't handle non-finite values.
Results may differ from a plain program's by a relative error of at most 0.0003.
Values may be sent and summed in bfloat16 or wider, within the bound.
A program may use at most 64 MiB of HBM per device.

v0:
```python
import math

import jax
import jax.numpy as jnp
from jax import lax
from jax.sharding import PartitionSpec as P

SUB = 8
K = 256


def code_sums(residual, code_pair):
    total_rows = residual.shape[0]
    subspaces = code_pair[0].shape[1]
    block_rows = math.gcd(total_rows, 32768 // subspaces)
    turn_count = total_rows // block_rows
    shaped = residual.reshape(turn_count, block_rows, subspaces, SUB)
    codewords = jnp.arange(K, dtype=jnp.int32)
    zeros_sums = jnp.zeros((subspaces, K, SUB), jnp.float32)
    zeros_counts = jnp.zeros((subspaces, K), jnp.float32)

    def add_block(running, block_index):
        row_block = lax.dynamic_index_in_dim(shaped, block_index, 0, keepdims=False)
        updated = []
        for code_all, state in zip(code_pair, running):
            code_block = lax.dynamic_slice_in_dim(code_all, block_index * block_rows, block_rows, 0)
            one_hot = (code_block[:, :, None] == codewords).astype(row_block.dtype)
            block_sums = jnp.einsum(
                "rsk,rsc->skc",
                one_hot,
                row_block,
                preferred_element_type=jnp.float32,
                precision=lax.Precision.HIGHEST,
            )
            block_counts = jnp.sum(one_hot, axis=0, dtype=jnp.float32)
            updated.append((state[0] + block_sums, state[1] + block_counts))
        return (tuple(updated), None)

    start_state = ((zeros_sums, zeros_counts), (zeros_sums, zeros_counts))
    final_state, unused = lax.scan(add_block, start_state, jnp.arange(turn_count, dtype=jnp.int32))
    laid_out = []
    for sums_part, counts_part in final_state:
        laid_out.append(jnp.transpose(sums_part, (1, 0, 2)).reshape(K, subspaces * SUB))
        laid_out.append(counts_part.T)
    return tuple(laid_out)


def finish(first_sums, first_counts, second_sums, second_counts):
    totals = lax.psum((first_sums, first_counts, second_sums, second_counts), "rep")
    codebooks = []
    for sums_part, counts_part in ((totals[0], totals[1]), (totals[2], totals[3])):
        spread = jnp.repeat(jnp.maximum(counts_part, 1.0), SUB, axis=1)
        codebooks.append(sums_part / spread)
    return (codebooks[0], codebooks[1])


def plan_slots(list_ids, list_place, shard_rows, devices, capacity):
    local_rows = list_ids.shape[0]
    places = jnp.take(list_place, list_ids, axis=0)
    owner_ids = places // shard_rows
    slot_in = places - owner_ids * shard_rows
    by_owner = jnp.argsort(owner_ids, stable=True)
    sorted_owner = owner_ids[by_owner]
    per_owner = jnp.sum(
        (owner_ids[:, None] == jnp.arange(devices, dtype=jnp.int32)[None, :]).astype(jnp.int32),
        axis=0,
    )
    first_row = jnp.cumsum(per_owner) - per_owner
    rank_sorted = jnp.arange(local_rows, dtype=jnp.int32) - first_row[sorted_owner]
    position = (
        jnp.zeros((local_rows,), jnp.int32).at[by_owner].set(sorted_owner * capacity + rank_sorted)
    )
    request = (
        jnp.zeros((devices * capacity,), jnp.int32)
        .at[position]
        .set(slot_in)
        .reshape(devices, capacity)
    )
    return (position, request)


def fetch_residual(vectors, centroids, position, request, devices, capacity):
    wanted_ids = lax.all_to_all(request, ("rows", "rep"), split_axis=0, concat_axis=0, tiled=True)
    answer = jnp.take(centroids, wanted_ids.reshape(-1), axis=0)
    answer = answer.reshape(wanted_ids.shape[0], wanted_ids.shape[1], centroids.shape[1])
    fetched = lax.all_to_all(answer, ("rows", "rep"), split_axis=0, concat_axis=0, tiled=True)
    fetched_rows = jnp.take(
        fetched.reshape(devices * capacity, centroids.shape[1]), position, axis=0
    )
    return vectors.astype(jnp.float32) - fetched_rows.astype(jnp.float32)


def on_device(vectors, list_ids, centroids, list_place, codes_first, codes_second):
    devices = lax.axis_size(("rows", "rep"))
    local_rows = vectors.shape[0]
    shard_rows = centroids.shape[0]
    capacity = 2 * local_rows // devices
    position, request = plan_slots(list_ids, list_place, shard_rows, devices, capacity)
    residual = fetch_residual(vectors, centroids, position, request, devices, capacity)
    transposed = (
        lax.all_to_all(residual, "rows", split_axis=1, concat_axis=0, tiled=True),
        lax.all_to_all(codes_first, "rows", split_axis=1, concat_axis=0, tiled=True),
        lax.all_to_all(codes_second, "rows", split_axis=1, concat_axis=0, tiled=True),
    )
    local_parts = code_sums(transposed[0], (transposed[1], transposed[2]))
    return finish(local_parts[0], local_parts[1], local_parts[2], local_parts[3])


def solution(mesh):
    return jax.shard_map(
        on_device,
        mesh=mesh,
        in_specs=(
            P(("rows", "rep"), None),
            P(("rows", "rep")),
            P(("rows", "rep"), None),
            P(),
            P(("rows", "rep"), None),
            P(("rows", "rep"), None),
        ),
        out_specs=(P(None, "rows"), P(None, "rows")),
        check_vma=False,
    )
```

profile of v0, /device:TPU:0, one launch (start us, length us, event | category | flops | bytes accessed | tf_op | source)
XLA Modules:
  0.0 313.5 jit_solution(9564695646376202633)
XLA Ops:
  7.2 0.8 compare_select_fusion.5
  8.4 3.1 gather_fusion
  12.2 3.8 %sort.17 = (s32[512]{0:T(512)}, s32[512]{0:T(512)S(1)}) sort(s32[512]{0:T(512)S(1)} %get-tuple-element.172, s32[512]{0:T(512)S(1)} %iota.21), dimensions={0}, to_apply=%region_0.1 | sort | flops 4608 | bytes 8192 | tf_op jit(solution)/shard_map/jit(argsort)/sort | solution.py:62
  15.9 3.5 %gather_fusion.1 = s32[512]{0:T(512)S(1)} fusion(s32[512]{0:T(512)S(1)} %get-tuple-element.172, s32[1024]{0:T(1024)S(1)} %pad_clamp_fusion.2), kind=kCustom, calls=%fused_computation.1 | custom fusion | bytes 6144 | tf_op jit(solution)/shard_map/gather | solution.py:63
  19.5 3.3 %gather_fusion.2 = s32[512]{0:T(512)S(1)} fusion(s32[128]{0:T(128)S(1)} %sub.19, s32[1024]{0:T(1024)S(1)} %pad_clamp_fusion.1), kind=kCustom, calls=%fused_computation.2 | custom fusion | bytes 6144 | tf_op jit(solution)/shard_map/gather | solution.py:69
  22.8 2.4 scatter_custom_fusion
  25.3 2.4 scatter_custom_fusion.1
  27.8 20.0 %all_to_all.68 = s32[128,1,8]{2,1,0:T(1,128)S(1)} all-to-all(s32[128,1,8]{2,1,0:T(1,128)S(1)} %bitcast.51), channel_id=1, replica_groups=mesh['rows'=32,'rep'=4] {'rows','rep'}, dimensions={0} | all-to-all | bytes 8192 | tf_op jit(solution)/shard_map/all_to_all | solution.py:83
  48.3 0.8 reduce.4
  49.3 7.7 %gather_fusion.3 = bf16[1024,1024]{1,0:T(8,128)(2,1)S(1)} fusion(bf16[2048,1024]{1,0:T(8,128)(2,1)} %param.10, s32[1024]{0:T(1024)S(1)} %broadcast_clamp_fusion), kind=kCustom, calls=%fused_computation.3 | custom fusion | bytes 4198400 | tf_op jit(solution)/shard_map/jit(_take)/gather | solution.py:84
  57.0 1.6 bitcast_select_fusion
  58.7 4.9 %all-to-all-start.2 = ((bf16[128,8,1024]{2,1,0:T(8,128)(2,1)}), bf16[128,8,1024]{2,1,0:T(8,128)(2,1)S(1)}, u32[]{:S(2)}, u32[]{:S(2)}) async-start(bf16[128,8,1024]{2,1,0:T(8,128)(2,1)} %bitcast_select_fusion), calls=%async_computation.2 | async-start | bytes 4194304 | tf_op jit(solution)/shard_map/all_to_all | solution.py:86
  63.6 1.1 copy.24
  64.6 0.8 all_to_all.49
  65.5 28.3 %all-to-all-done.2 = bf16[128,8,1024]{2,1,0:T(8,128)(2,1)S(1)} async-done(((bf16[128,8,1024]{2,1,0:T(8,128)(2,1)}), bf16[128,8,1024]{2,1,0:T(8,128)(2,1)S(1)}, u32[]{:S(2)}, u32[]{:S(2)}) %all-to-all-start.2) | async-done | bytes 2097184 | tf_op jit(solution)/shard_map/all_to_all | solution.py:86
  93.7 3.9 %all-to-all-start = ((s32[512,32,4]{0,2,1:T(4,128)}), s32[512,32,4]{0,2,1:T(4,128)S(1)}, u32[]{:S(2)}, u32[]{:S(2)}) async-start(s32[512,32,4]{0,2,1:T(4,128)} %all_to_all.49), calls=%async_computation | async-start | bytes 524288 | tf_op jit(solution)/shard_map/all_to_all | solution.py:102
  97.6 2.8 gather_fusion.4
  100.4 1.9 convert_subtract_fusion
  102.3 1.9 copy.27
  104.2 2.4 all-to-all-done
  106.5 5.0 %all-to-all-start.3 = ((f32[512,32,32]{0,2,1:T(8,128)}), f32[512,32,32]{0,2,1:T(8,128)S(1)}, u32[]{:S(2)}, u32[]{:S(2)}) async-start(f32[512,32,32]{0,2,1:T(8,128)} %bitcast.48), calls=%async_computation.3 | async-start | bytes 4194304 | tf_op jit(solution)/shard_map/all_to_all | solution.py:101
  111.5 1.8 copy.29
  113.4 1.7 all_to_all.59
  115.1 25.4 %all-to-all-done.3 = f32[512,32,32]{0,2,1:T(8,128)S(1)} async-done(((f32[512,32,32]{0,2,1:T(8,128)}), f32[512,32,32]{0,2,1:T(8,128)S(1)}, u32[]{:S(2)}, u32[]{:S(2)}) %all-to-all-start.3) | async-done | bytes 2097184 | tf_op jit(solution)/shard_map/all_to_all | solution.py:101
  140.5 4.6 %all-to-all-start.4 = ((s32[512,32,4]{0,2,1:T(4,128)}), s32[512,32,4]{0,2,1:T(4,128)}, u32[]{:S(2)}, u32[]{:S(2)}) async-start(s32[512,32,4]{0,2,1:T(4,128)} %all_to_all.59), calls=%async_computation.4 | async-start | bytes 524288 | tf_op jit(solution)/shard_map/all_to_all | solution.py:103
  145.3 2.5 copy.28
  147.8 4.0 %reshape.159 = f32[2,8192,4,8]{1,0,3,2:T(2,128)} reshape(f32[32,512,32]{1,0,2:T(8,128)} %copy.28) | data formatting | bytes 4194304 | tf_op jit(solution)/shard_map/reshape | solution.py:17
  151.9 2.1 all-to-all-done.4
  154.0 111.4 %while.18 = (s32[]{:T(128)}, f32[4,256,8]{1,2,0:T(8,128)S(1)}, f32[4,256]{1,0:T(4,128)S(1)}, f32[4,256,8]{1,2,0:T(8,128)S(1)}, f32[4,256]{1,0:T(4,128)S(1)}, /*i...) while((s32[]{:T(128)}, f32[4,256,8]{1,2,0:T(8,128)S(1)}, ...), condition=%wide.region_8.9_spmd.clone.clone, body=%wide.region_5.8_spmd.clone.clone.sunk | while | flops 1677756416 | bytes 5406969 | solution.py:40
  154.0 0.6 dynamic_slice.32
  155.2 0.9 constant_dynamic-slice_fusion.8
  158.1 2.7 constant_dynamic-slice_fusion.7
  160.8 10.9 %fusion.25 = f32[4,256,8]{1,2,0:T(8,128)S(1)} fusion(s32[8192,4]{0,1:T(4,128)S(1)} %constant_dynamic-slice_fusion.8, f32[1,8192,4,8]{1,0,3,2:T(1,128)S(1)} %constant_dynamic-slice_fusion.7, f32[4,256,8]{1,2,0:T(8,128)S(1)} %get-tuple-element.253, pred[]{:T(512)S(6)} %compare.12), kind=kOutput, calls=%fused_computation.18.clone.1 | convolution fusion | flops 813711360 | bytes 1245185 | tf_op jit(solution)/shard_map/while/body/eval_jaxpr/rsk,rsc->skc/dot_general | solution.py:28
  171.7 10.9 %fusion.22 = f32[4,256,8]{1,2,0:T(8,128)S(1)} fusion(s32[8192,4]{0,1:T(4,128)S(1)} %constant_dynamic-slice_fusion.6, f32[1,8192,4,8]{1,0,3,2:T(1,128)S(1)} %constant_dynamic-slice_fusion.7, f32[4,256,8]{1,2,0:T(8,128)S(1)} %get-tuple-element.251, pred[]{:T(512)S(6)} %compare.12), kind=kOutput, calls=%fused_computation.19.clone.1 | convolution fusion | flops 813711360 | bytes 1245185 | tf_op jit(solution)/shard_map/while/body/eval_jaxpr/rsk,rsc->skc/dot_general | solution.py:28
  182.5 13.5 %fusion.23 = f32[4,256]{1,0:T(4,128)S(1)} fusion(s32[8192,4]{0,1:T(4,128)S(1)} %constant_dynamic-slice_fusion.8), kind=kLoop, calls=%fused_computation.14.clone.1 | loop fusion | flops 25164800 | bytes 135168 | tf_op jit(solution)/shard_map/while/body/eval_jaxpr/reduce_sum | solution.py:35
  196.1 13.6 %fusion.24 = f32[4,256]{1,0:T(4,128)S(1)} fusion(s32[8192,4]{0,1:T(4,128)S(1)} %constant_dynamic-slice_fusion.6), kind=kLoop, calls=%fused_computation.15.clone.1 | loop fusion | flops 25164800 | bytes 135168 | tf_op jit(solution)/shard_map/while/body/eval_jaxpr/reduce_sum | solution.py:35
  209.7 0.6 dynamic_slice.32
  211.0 0.9 constant_dynamic-slice_fusion.8
  213.8 2.7 constant_dynamic-slice_fusion.7
  216.5 10.9 %fusion.25 = f32[4,256,8]{1,2,0:T(8,128)S(1)} fusion(s32[8192,4]{0,1:T(4,128)S(1)} %constant_dynamic-slice_fusion.8, f32[1,8192,4,8]{1,0,3,2:T(1,128)S(1)} %constant_dynamic-slice_fusion.7, f32[4,256,8]{1,2,0:T(8,128)S(1)} %get-tuple-element.253, pred[]{:T(512)S(6)} %compare.12), kind=kOutput, calls=%fused_computation.18.clone.1 | convolution fusion | flops 813711360 | bytes 1245185 | tf_op jit(solution)/shard_map/while/body/eval_jaxpr/rsk,rsc->skc/dot_general | solution.py:28
  227.4 10.9 %fusion.22 = f32[4,256,8]{1,2,0:T(8,128)S(1)} fusion(s32[8192,4]{0,1:T(4,128)S(1)} %constant_dynamic-slice_fusion.6, f32[1,8192,4,8]{1,0,3,2:T(1,128)S(1)} %constant_dynamic-slice_fusion.7, f32[4,256,8]{1,2,0:T(8,128)S(1)} %get-tuple-element.251, pred[]{:T(512)S(6)} %compare.12), kind=kOutput, calls=%fused_computation.19.clone.1 | convolution fusion | flops 813711360 | bytes 1245185 | tf_op jit(solution)/shard_map/while/body/eval_jaxpr/rsk,rsc->skc/dot_general | solution.py:28
  238.3 13.5 %fusion.23 = f32[4,256]{1,0:T(4,128)S(1)} fusion(s32[8192,4]{0,1:T(4,128)S(1)} %constant_dynamic-slice_fusion.8), kind=kLoop, calls=%fused_computation.14.clone.1 | loop fusion | flops 25164800 | bytes 135168 | tf_op jit(solution)/shard_map/while/body/eval_jaxpr/reduce_sum | solution.py:35
  251.8 13.6 %fusion.24 = f32[4,256]{1,0:T(4,128)S(1)} fusion(s32[8192,4]{0,1:T(4,128)S(1)} %constant_dynamic-slice_fusion.6), kind=kLoop, calls=%fused_computation.15.clone.1 | loop fusion | flops 25164800 | bytes 135168 | tf_op jit(solution)/shard_map/while/body/eval_jaxpr/reduce_sum | solution.py:35
  265.5 0.6 copy-done.1
  266.1 37.8 %all-reduce.3.cloned.1.call-done = (f32[256,32]{0,1:T(8,128)}, f32[256,4]{0,1:T(4,128)}, f32[256,32]{0,1:T(8,128)}, f32[256,4]{0,1:T(4,128)}) async-done(((f32[256,32]{0,1:T(8,128)}, f32[256,4]{0,1:T(4,128)}, f32[256,32]{0,1:T(8,128)}, f32[256,4]{0,1:T(4,128)}), (f32[256,32]{0,1:T(8,128)}, f32[256,4]{0,1:T(4,128)}, f32[256,32]{0,1:T(8,128)}, f32[256,4]{0,1:T(4,128)})) %all-reduce.3.cloned.1.call-update) | async-done | bytes 73744 | tf_op jit(solution)/shard_map/psum | solution.py:49
  303.9 0.7 broadcast_maximum_fusion
  304.6 0.7 broadcast_maximum_fusion.1
  305.2 1.4 bitcast_divide_fusion
  (44 shorter events, 2.2 us)
Async XLA Ops:
  7.2 1.2 copy-start
  7.2 4.4 %copy-start.5 = (s32[512]{0:T(512)S(1)}, s32[512]{0:T(512)}, u32[]{:S(2)}) copy-start(s32[512]{0:T(512)} %param.9) | copy-start | bytes 6148
  58.7 35.1 %all-to-all-start.2 = ((bf16[128,8,1024]{2,1,0:T(8,128)(2,1)}), bf16[128,8,1024]{2,1,0:T(8,128)(2,1)S(1)}, u32[]{:S(2)}, u32[]{:S(2)}) async-start(bf16[128,8,1024]{2,1,0:T(8,128)(2,1)} %bitcast_select_fusion), calls=%async_computation.2 | async-start | bytes 4194304 | tf_op jit(solution)/shard_map/all_to_all | solution.py:86
  93.7 12.8 %all-to-all-start = ((s32[512,32,4]{0,2,1:T(4,128)}), s32[512,32,4]{0,2,1:T(4,128)S(1)}, u32[]{:S(2)}, u32[]{:S(2)}) async-start(s32[512,32,4]{0,2,1:T(4,128)} %all_to_all.49), calls=%async_computation | async-start | bytes 524288 | tf_op jit(solution)/shard_map/all_to_all | solution.py:102
  106.5 33.9 %all-to-all-start.3 = ((f32[512,32,32]{0,2,1:T(8,128)}), f32[512,32,32]{0,2,1:T(8,128)S(1)}, u32[]{:S(2)}, u32[]{:S(2)}) async-start(f32[512,32,32]{0,2,1:T(8,128)} %bitcast.48), calls=%async_computation.3 | async-start | bytes 4194304 | tf_op jit(solution)/shard_map/all_to_all | solution.py:101
  140.5 13.5 %all-to-all-start.4 = ((s32[512,32,4]{0,2,1:T(4,128)}), s32[512,32,4]{0,2,1:T(4,128)}, u32[]{:S(2)}, u32[]{:S(2)}) async-start(s32[512,32,4]{0,2,1:T(4,128)} %all_to_all.59), calls=%async_computation.4 | async-start | bytes 524288 | tf_op jit(solution)/shard_map/all_to_all | solution.py:103
  145.1 158.8 %all-reduce.3.cloned.1.call-start = ((), (), s32[]{:S(2)}) async-start(), calls=%async_computation.5 | async-start | bytes 147456 | tf_op jit(solution)/shard_map/psum | solution.py:49
  265.4 0.6 copy-start.1
  265.4 0.6 copy-start.2
  265.4 0.6 copy-start.3
  265.5 0.6 copy-start.4
Sparse Core Ops, SparseCore 0:
  266.2 37.6 all-reduce.2
where the time goes:
time: 314 us
  waiting for transfers between devices  95.9 us (31%)
  other arithmetic  66.5 us (21%)
  local copies, waits for them, and re-layouts  49.5 us (16%)
  matrix products  43.4 us (14%)
  blocking collectives  20 us (6%)
  starting transfers between devices  18.6 us (6%)
  between operations  14.3 us (5%)
  loops' own time  5.27 us (2%)
    reduce_sum x4, other arithmetic, add_block(): block_counts = jnp.sum(one_hot, axis=0, dtype=jnp.float32)  54.3 us
    dot_general x4, matrix products, add_block(): jnp.einsum('rsk,rsc->skc', one_hot, row_block, preferred_element_type=jnp...  43.4 us
    psum x1, waiting for transfers between devices, finish(): lax.psum((first_sums, first_counts, second_sums, second_counts), 'rep')  37.8 us
    all_to_all x1, waiting for transfers between devices, fetch_residual(): lax.all_to_all(answer, ('rows', 'rep'), split_axis=0, concat_axis=0, tile...  28.3 us
    all_to_all x1, waiting for transfers between devices, on_device(): lax.all_to_all(residual, 'rows', split_axis=1, concat_axis=0, tiled=True)  25.4 us
    all_to_all x1, blocking collectives, fetch_residual(): lax.all_to_all(request, ('rows', 'rep'), split_axis=0, concat_axis=0, til...  20 us
    gather x1, local copies, waits for them, and re-layouts, fetch_residual(): answer = jnp.take(centroids, wanted_ids.reshape(-1), axis=0)  7.71 us
  transfers between devices with their start and end apart: 5, of which 5 were waited for; matrix products, arithmetic and copies ran while one was open for 5% of the time, Pallas kernels for 0%

commit v1 on v0

v1 whole, which is shorter than its diff:
```python
import functools

import jax
import jax.numpy as jnp
from jax import lax
from jax.experimental import pallas as pl
from jax.experimental.pallas import tpu as pltpu
from jax.sharding import PartitionSpec as P

SUB = 8
K = 256
DEV = 128
CAP = 8
ROWS_DEV = 512
CENT_DEV = 2048
S = 128
D = 1024
MESH = pl.DeviceIdType.MESH
F32 = jnp.float32
BF16 = jnp.bfloat16


def iota(shape, dim):
    return lax.broadcasted_iota(jnp.int32, shape, dim)


def nt(a, b):
    return lax.dot_general(a, b, (((1,), (1,)), ((), ())), preferred_element_type=F32)


def nn(a, b):
    return jnp.dot(a, b, preferred_element_type=F32)


def one_hot(match, dtype=BF16):
    return jnp.where(match, 1.0, 0.0).astype(dtype)


def exchange_kernel(ids, place, first, second, recv, found, send, send_sem, recv_sem):
    rows_at = lax.axis_index("rows")
    rep_at = lax.axis_index("rep")
    me = rows_at * 4 + rep_at
    barrier = pltpu.get_barrier_semaphore()

    def greet(step, unused):
        other = lax.rem(me + step, DEV)
        pl.semaphore_signal(
            barrier, inc=1, device_id=(other // 4, lax.rem(other, 4)), device_id_type=MESH
        )
        return unused

    lax.fori_loop(1, DEV, greet, 0)

    lanes = iota((1, 128), 1)

    def find(block, unused):
        for step in range(8):
            row = block * 8 + step
            wanted = ids[row]
            found[pl.ds(row, 1), :] = jnp.where(
                lanes == (wanted & 127), place[pl.ds(wanted >> 7, 1), :], 0
            )
        return unused

    lax.fori_loop(0, ROWS_DEV // 8, find, 0)

    places = found[...]
    owner = (places >> 11).astype(F32).astype(BF16)
    slot_high = ((places >> 7) & 15).astype(F32).astype(BF16)
    slot_low = (places & 127).astype(F32).astype(BF16)
    owner_row = nt(jnp.ones((8, 128), BF16), owner)[0:1, :].astype(jnp.int32)
    owner_is = iota((DEV, ROWS_DEV), 0) == owner_row
    earlier = one_hot(iota((ROWS_DEV, ROWS_DEV), 0) < iota((ROWS_DEV, ROWS_DEV), 1))
    before = nn(one_hot(owner_is), earlier)
    rank = jnp.sum(jnp.where(owner_is, before, 0.0), axis=0, keepdims=True)
    position = owner_row * CAP + rank.astype(jnp.int32)
    move = one_hot(iota((DEV * CAP, ROWS_DEV), 0) == position)
    ones = jnp.ones((128, 128), BF16)
    payload = jnp.concatenate(
        [
            (first[...] + 1).astype(F32).astype(BF16),
            (second[...] + 1).astype(F32).astype(BF16),
            nn(slot_high, ones).astype(BF16),
            nn(slot_low, ones).astype(BF16),
        ],
        axis=1,
    )
    moved = nn(move, payload).astype(jnp.int32)
    codes = moved[:, 0:128] + moved[:, 128:256] * 65536
    slots = moved[:, 256:384] * 128 + moved[:, 384:512]
    send[:, 0:8, :] = codes.reshape(DEV, CAP, 128)
    send[:, 8:16, :] = slots.reshape(DEV, CAP, 128)

    pl.semaphore_wait(barrier, DEV - 1)

    def push(step, unused):
        other = lax.rem(me + step, DEV)
        pltpu.make_async_remote_copy(
            src_ref=send.at[other],
            dst_ref=recv.at[step],
            send_sem=send_sem,
            recv_sem=recv_sem,
            device_id=(other // 4, lax.rem(other, 4)),
            device_id_type=MESH,
        ).start()
        return unused

    lax.fori_loop(1, DEV, push, 0)
    recv[0] = send[me]
    rest = recv.at[pl.ds(1, DEV - 1)]
    pltpu.make_async_copy(rest, rest, recv_sem).wait()
    pltpu.make_async_copy(rest, rest, send_sem).wait()


def exchange(ids, place, first, second):
    return pl.pallas_call(
        exchange_kernel,
        out_shape=jax.ShapeDtypeStruct((DEV, 16, 128), jnp.int32),
        in_specs=[pl.BlockSpec(memory_space=pltpu.SMEM)]
        + [pl.BlockSpec(memory_space=pltpu.VMEM)] * 3,
        out_specs=pl.BlockSpec(memory_space=pltpu.VMEM),
        scratch_shapes=[
            pltpu.VMEM((ROWS_DEV, 128), jnp.int32),
            pltpu.VMEM((DEV, 16, 128), jnp.int32),
            pltpu.SemaphoreType.DMA,
            pltpu.SemaphoreType.DMA,
        ],
        compiler_params=pltpu.CompilerParams(
            collective_id=0, has_side_effects=True, vmem_limit_bytes=40 * 2**20
        ),
        name="exchange",
    )(ids, place, first, second)


ALL_ROWS = ROWS_DEV + DEV * CAP
CHUNK = 256


def sums_kernel(vectors, first, second, recv, table, out, spread, high, low):
    at = iota((512, 256), 0)
    pick = ((at >> 4) * 8 + (at & 7)) == iota((512, 256), 1)
    plus = one_hot(pick)
    minus = -plus
    eye = one_hot(iota((128, 128), 0) == iota((128, 128), 1))

    def lay_codes(codes_column, index, start):
        turned = nt(eye, codes_column.astype(F32).astype(BF16)) - 1.0
        high_part = jnp.floor(turned * 0.125)
        high[index, :, start : start + CHUNK] = high_part
        low[index, :, start : start + CHUNK] = turned - 8.0 * high_part

    for part in range(ROWS_DEV // CHUNK):
        start = part * CHUNK
        for block in range(D // 256):
            cut = vectors[start : start + CHUNK, block * 256 : (block + 1) * 256]
            spread[block * 512 : (block + 1) * 512, start : start + CHUNK] = nt(plus, cut).astype(BF16)
        lay_codes(first[start : start + CHUNK, :] + 1, 0, start)
        lay_codes(second[start : start + CHUNK, :] + 1, 1, start)

    for part in range(DEV * CAP // CHUNK):
        start = ROWS_DEV + part * CHUNK
        sources = CHUNK // CAP
        block_codes = recv[part * sources : (part + 1) * sources, 0:8, :].reshape(CHUNK, 128)
        slots = recv[part * sources : (part + 1) * sources, 8:16, :].reshape(CHUNK, 128)
        lay_codes(block_codes & 65535, 0, start)
        lay_codes(block_codes >> 16, 1, start)
        wanted = jnp.concatenate(
            [
                one_hot(slots == iota((CHUNK, 128), 1) + 128 * j)
                for j in range(CENT_DEV // 128)
            ],
            axis=1,
        )
        base = nn(wanted, table[...]).astype(BF16)
        for block in range(D // 256):
            cut = base[:, block * 256 : (block + 1) * 256]
            spread[block * 512 : (block + 1) * 512, start : start + CHUNK] = nt(minus, cut).astype(BF16)

    high_is = iota((32, CHUNK), 0).astype(F32).astype(BF16)
    low_is = (iota((64, CHUNK), 0) >> 3).astype(F32).astype(BF16)
    count_at = iota((16, CHUNK), 0)
    count_is = jnp.where(count_at < 8, count_at, -5).astype(F32).astype(BF16)
    lane_of = iota((32, 256), 1) >> 6
    count_lane_of = iota((32, 64), 1) >> 4
    one = jnp.ones((), BF16)
    zero = jnp.zeros((), BF16)

    def owner_step(owner, unused):
        counted = []
        core, spot = lax.rem(owner, 2), owner // 2
        for index in range(2):
            total = jnp.zeros((128, 256), F32)
            count = jnp.zeros((128, 64), F32)
            for part in range(ALL_ROWS // CHUNK):
                start = part * CHUNK
                left, right, mark = [], [], []
                for sub in range(4):
                    at_sub = owner * 4 + sub
                    h = high[index, pl.ds(at_sub, 1), start : start + CHUNK].astype(BF16)
                    l = low[index, pl.ds(at_sub, 1), start : start + CHUNK].astype(BF16)
                    data = spread[
                        pl.ds(pl.multiple_of(at_sub * 16, 16), 16), start : start + CHUNK
                    ]
                    left.append(jnp.where(high_is == h, one, zero))
                    four = jnp.concatenate([data] * 4, axis=0)
                    right.append(jnp.where(low_is == l, four, zero))
                    if part < ROWS_DEV // CHUNK:
                        mark.append(jnp.where(count_is == l, one, zero))
                left = jnp.concatenate(left, axis=0)
                total = total + nt(left, jnp.concatenate(right, axis=0))
                if part < ROWS_DEV // CHUNK:
                    count = count + nt(left, jnp.concatenate(mark, axis=0))
            mine = jnp.zeros((32, 256), F32)
            mine_count = jnp.zeros((32, 64), F32)
            for sub in range(4):
                mine = jnp.where(lane_of == sub, total[32 * sub : 32 * sub + 32, :], mine)
                mine_count = jnp.where(
                    count_lane_of == sub, count[32 * sub : 32 * sub + 32, :], mine_count
                )
            out[core, spot, :, 2 * index] = mine[:, 0:128].reshape(4, 8, 128)
            out[core, spot, :, 2 * index + 1] = mine[:, 128:256].reshape(4, 8, 128)
            counted.append(mine_count)
        out[core, spot, :, 4] = jnp.concatenate(counted, axis=1).reshape(4, 8, 128)
        return unused

    lax.fori_loop(0, 32, owner_step, 0)


def local_sums(vectors, first, second, recv, table):
    return pl.pallas_call(
        sums_kernel,
        out_shape=jax.ShapeDtypeStruct((2, 16, 4, 5, 8, 128), F32),
        in_specs=[pl.BlockSpec(memory_space=pltpu.VMEM)] * 5,
        out_specs=pl.BlockSpec(memory_space=pltpu.VMEM),
        scratch_shapes=[
            pltpu.VMEM((2 * D, ALL_ROWS), BF16),
            pltpu.VMEM((2, S, ALL_ROWS), F32),
            pltpu.VMEM((2, S, ALL_ROWS), F32),
        ],
        compiler_params=pltpu.CompilerParams(vmem_limit_bytes=50 * 2**20),
        name="local_sums",
    )(vectors, first, second, recv, table)


def reduce_kernel(
    parts, out, mate, half, landed, core_send, core_recv, part_send, part_recv, last_send, last_recv
):
    rows_at = lax.axis_index("rows")
    z = lax.axis_index("rep")
    core = lax.rem(rows_at, 2)
    y = lax.rem(rows_at // 2, 4)
    x = rows_at // 8
    barrier = pltpu.get_barrier_semaphore()

    def place_of(step):
        x_to = lax.rem(x + step // 16, 4)
        y_to = lax.rem(y + lax.rem(step // 4, 4), 4)
        z_to = lax.rem(z + lax.rem(step, 4), 4)
        return x_to * 4 + y_to, z_to

    mate_id = (rows_at + 1 - 2 * core, z)
    pl.semaphore_signal(barrier, inc=1, device_id=mate_id, device_id_type=MESH)

    def greet(step, unused):
        spot, z_to = place_of(step)
        pl.semaphore_signal(
            barrier, inc=1, device_id=(spot * 2 + core, z_to), device_id_type=MESH
        )
        return unused

    lax.fori_loop(1, 64, greet, 0)
    pl.semaphore_wait(barrier, 64)

    def core_copy(step):
        spot, unused = place_of(step * 4)
        return pltpu.make_async_remote_copy(
            src_ref=parts.at[1 - core, spot],
            dst_ref=mate.at[step],
            send_sem=core_send.at[step],
            recv_sem=core_recv.at[step],
            device_id=mate_id,
            device_id_type=MESH,
        )

    def start_core(step, unused):
        core_copy(lax.rem(step, 16)).start()
        return unused

    lax.fori_loop(1, 17, start_core, 0)

    def part_copy(step):
        spot, z_to = place_of(step)
        return pltpu.make_async_remote_copy(
            src_ref=half.at[step // 4, z_to],
            dst_ref=landed.at[step],
            send_sem=part_send,
            recv_sem=part_recv,
            device_id=(spot * 2 + core, z_to),
            device_id_type=MESH,
        )

    def send_parts(turn, unused):
        step = lax.rem(turn, 16)
        core_copy(step).wait_recv()
        spot, unused_z = place_of(step * 4)
        half[step] = parts[core, spot] + mate[step]

        @pl.when(step != 0)
        def _():
            part_copy(step * 4).start()

        for z_step in range(1, 4):
            part_copy(step * 4 + z_step).start()
        return unused

    lax.fori_loop(1, 17, send_parts, 0)

    rest = landed.at[pl.ds(1, 63)]
    pltpu.make_async_copy(rest, rest, part_recv).wait()

    def add(step, total):
        return total + landed[step]

    out[z] = lax.fori_loop(1, 64, add, half[0, z])

    for z_step in range(1, 4):
        pltpu.make_async_remote_copy(
            src_ref=out.at[z],
            dst_ref=out.at[z],
            send_sem=last_send,
            recv_sem=last_recv,
            device_id=(rows_at, lax.rem(z + z_step, 4)),
            device_id_type=MESH,
        ).start()
    three = landed.at[pl.ds(0, 3)]
    pltpu.make_async_copy(three, three, last_recv).wait()
    pltpu.make_async_copy(three, three, last_send).wait()
    pltpu.make_async_copy(rest, rest, part_send).wait()

    def end_core(step, unused):
        core_copy(step).wait_send()
        return unused

    lax.fori_loop(0, 16, end_core, 0)


def reduce_parts(parts):
    return pl.pallas_call(
        reduce_kernel,
        out_shape=jax.ShapeDtypeStruct((4, 5, 8, 128), F32),
        in_specs=[pl.BlockSpec(memory_space=pltpu.VMEM)],
        out_specs=pl.BlockSpec(memory_space=pltpu.VMEM),
        scratch_shapes=[
            pltpu.VMEM((16, 4, 5, 8, 128), F32),
            pltpu.VMEM((16, 4, 5, 8, 128), F32),
            pltpu.VMEM((64, 5, 8, 128), F32),
            pltpu.SemaphoreType.DMA((16,)),
            pltpu.SemaphoreType.DMA((16,)),
            pltpu.SemaphoreType.DMA,
            pltpu.SemaphoreType.DMA,
            pltpu.SemaphoreType.DMA,
            pltpu.SemaphoreType.DMA,
        ],
        compiler_params=pltpu.CompilerParams(
            collective_id=1, has_side_effects=True, vmem_limit_bytes=40 * 2**20
        ),
        name="reduce_parts",
    )(parts)


def means_kernel(total, out_first, out_second):
    count = jnp.maximum(total[:, 4].reshape(32, 128), 1.0)
    for index, out in ((0, out_first), (1, out_second)):
        sums = jnp.concatenate(
            [total[:, 2 * index].reshape(32, 128), total[:, 2 * index + 1].reshape(32, 128)], axis=1
        )
        from_lane = iota((128, 256), 0)
        lane = iota((128, 256), 1)
        fan = one_hot(from_lane == index * 64 + (lane >> 6) * 16 + ((lane >> 3) & 7), F32)
        fanned = jnp.dot(count, fan, preferred_element_type=F32, precision=lax.Precision.HIGHEST)
        means = sums / fanned
        wide = iota((256, 32), 0)
        column = iota((256, 32), 1)
        for low in range(8):
            choose = one_hot(wide == (column >> 3) * 64 + low * 8 + (column & 7), F32)
            out[pl.ds(low, 32, stride=8), :] = jnp.dot(
                means, choose, preferred_element_type=F32, precision=lax.Precision.HIGHEST
            )


def means_of(total):
    return pl.pallas_call(
        means_kernel,
        out_shape=[jax.ShapeDtypeStruct((K, 32), F32)] * 2,
        in_specs=[pl.BlockSpec(memory_space=pltpu.VMEM)],
        out_specs=[pl.BlockSpec(memory_space=pltpu.VMEM)] * 2,
        name="means",
    )(total)


def on_device(vectors, list_ids, centroids, list_place, codes_first, codes_second):
    place = list_place.reshape(2048, 128)
    recv = exchange(list_ids, place, codes_first, codes_second)
    parts = local_sums(vectors, codes_first, codes_second, recv, centroids)
    first, second = means_of(reduce_parts(parts))
    return (first, second)


def solution(mesh):
    return jax.shard_map(
        on_device,
        mesh=mesh,
        in_specs=(
            P(("rows", "rep"), None),
            P(("rows", "rep")),
            P(("rows", "rep"), None),
            P(),
            P(("rows", "rep"), None),
            P(("rows", "rep"), None),
        ),
        out_specs=(P(None, "rows"), P(None, "rows")),
        check_vma=False,
    )
```

time: 314 us -> 113 us (0.36)
  Pallas kernels: 0 us -> 98.5 us
  waiting for transfers between devices: 95.9 us -> 0 us
  other arithmetic: 66.5 us -> 0 us
  matrix products: 43.4 us -> 0 us
  local copies, waits for them, and re-layouts: 49.5 us -> 12.5 us
  blocking collectives: 20 us -> 0 us
  starting transfers between devices: 18.6 us -> 0 us
  between operations: 14.3 us -> 0.68 us
  loops' own time: 5.27 us -> 0 us
    pallas_call x0 -> x4, Pallas kernels: none -> 98.5 us  [the longest x1 38 us: reduce_parts(): pl.pallas_call(reduce_kernel, out_shape=jax.ShapeDtypeStruct((4, 5, 8, 12...]
    all_to_all x4 -> x0, waiting for transfers between devices: 58.1 us -> none  [the longest x1 28.3 us: fetch_residual(): lax.all_to_all(answer, ('rows', 'rep'), split_axis=0, concat_axis=0, tile...]
    reduce_sum x5 -> x0, other arithmetic: 54.4 us -> none  [the longest x4 54.3 us: add_block(): block_counts = jnp.sum(one_hot, axis=0, dtype=jnp.float32)]
    dot_general x4 -> x0, matrix products: 43.4 us -> none  [add_block(): jnp.einsum('rsk,rsc->skc', one_hot, row_block, preferred_element_type=jnp...]
    psum x1 -> x0, waiting for transfers between devices: 37.8 us -> none  [finish(): lax.psum((first_sums, first_counts, second_sums, second_counts), 'rep')]
    gather x5 -> x0, local copies, waits for them, and re-layouts: 20.5 us -> none  [the longest x1 7.71 us: fetch_residual(): answer = jnp.take(centroids, wanted_ids.reshape(-1), axis=0)]
    all_to_all x1 -> x0, blocking collectives: 20 us -> none  [fetch_residual(): lax.all_to_all(request, ('rows', 'rep'), split_axis=0, concat_axis=0, til...]
    all_to_all x4 -> x0, starting transfers between devices: 18.4 us -> none  [the longest x1 5.01 us: on_device(): lax.all_to_all(residual, 'rows', split_axis=1, concat_axis=0, tiled=True)]
  transfers between devices with their start and end apart: 5 -> 0, of which waited for: 5 -> 0; matrix products, arithmetic and copies ran while one was open for 5% -> 0% of each run, Pallas kernels for 0% -> 0%
where the time goes in v1:
time: 113 us; the launch traced here: 112 us
  Pallas kernels  98.5 us (87%)
  local copies, waits for them, and re-layouts  12.5 us (11%)
    pallas_call x1, Pallas kernels, reduce_parts(): pl.pallas_call(reduce_kernel, out_shape=jax.ShapeDtypeStruct((4, 5, 8, 12...  38 us
    pallas_call x1, Pallas kernels, local_sums(): pl.pallas_call(sums_kernel, out_shape=jax.ShapeDtypeStruct((2, 16, 4, 5,...  32.1 us
    pallas_call x1, Pallas kernels, exchange(): pl.pallas_call(exchange_kernel, out_shape=jax.ShapeDtypeStruct((DEV, 16,...  25.4 us
    unnamed x18, local copies, waits for them, and re-layouts  9.28 us
    pallas_call x2, local copies, waits for them, and re-layouts, means_of(): pl.pallas_call(means_kernel, out_shape=[jax.ShapeDtypeStruct((K, 32), F32...  3.19 us
    pallas_call x1, Pallas kernels, means_of(): pl.pallas_call(means_kernel, out_shape=[jax.ShapeDtypeStruct((K, 32), F32...  3.04 us

profile of v1, /device:TPU:0, one launch (start us, length us, event | category | flops | bytes accessed | tf_op | source)
XLA Modules:
  0.0 111.6 jit_solution(11287111381424192420)
XLA Ops:
  0.6 0.0 copy-start.2
  0.6 0.9 copy-done.2
  1.6 0.0 copy-start.4
  1.6 0.9 copy-done.4
  2.5 0.0 copy-start.6
  2.5 1.2 %copy-done.6 = s32[262144]{0:T(1024)S(1)} copy-done((s32[262144]{0:T(1024)S(1)}, s32[262144]{0:T(1024)}, u32[]{:S(2)}) %copy-start.6) | copy-done | bytes 1048600
  3.8 0.0 copy-start.8
  3.8 0.7 copy-done.8
  4.4 25.4 %exchange.1.recv = s32[128,16,128]{2,1,0:T(8,128)S(1)} custom-call(s32[512]{0:T(512)S(1)} %copy-done.8, s32[2048,128]{1,0:T(8,128)S(1)} %bitcast.1, s32[512,128]{1,0:T(8,128)S(1)} %copy-done.2, s32[512,128]{1,0:T(8,128)S(1)} %copy-done.4), custom_call_target="tpu_custom_call" | custom-call | tf_op jit(solution)/shard_map/exchange/pallas_call | solution.py:116
  29.8 0.0 copy-start.1
  29.9 1.2 %copy-done.1 = bf16[512,1024]{1,0:T(8,128)(2,1)S(1)} copy-done((bf16[512,1024]{1,0:T(8,128)(2,1)S(1)}, bf16[512,1024]{1,0:T(8,128)(2,1)}, u32[]{:S(2)}) %copy-start.1) | copy-done | bytes 1048600
  31.1 0.0 copy-start.3
  31.1 0.9 copy-done.3
  32.0 0.0 copy-start.5
  32.0 0.9 copy-done.5
  33.0 32.1 %local_sums.1.parts = f32[2,16,4,5,8,128]{5,4,3,2,1,0:T(8,128)} custom-call(bf16[512,1024]{1,0:T(8,128)(2,1)S(1)} %copy-done.1, s32[512,128]{1,0:T(8,128)S(1)} %copy-done.3, s32[512,128]{1,0:T(8,128)S(1)} %copy-done.5, s32[128,16,128]{2,1,0:T(8,128)S(1)} %exchange.1.recv, bf16[2048,1024]{1,0:T(8,128)(2,1)} %table.1), custom_call_target="tpu_custom_call" | custom-call | tf_op jit(solution)/shard_map/local_sums/pallas_call | solution.py:230
  65.1 0.0 copy-start
  65.1 1.7 %copy-done = f32[2,16,4,5,8,128]{5,4,3,2,1,0:T(8,128)S(1)} copy-done((f32[2,16,4,5,8,128]{5,4,3,2,1,0:T(8,128)S(1)}, f32[2,16,4,5,8,128]{5,4,3,2,1,0:T(8,128)}, u32[]{:S(2)}) %copy-start) | copy-done | bytes 2621464
  66.8 38.0 %reduce_parts.1.total = f32[4,5,8,128]{3,2,1,0:T(8,128)S(1)} custom-call(f32[2,16,4,5,8,128]{5,4,3,2,1,0:T(8,128)S(1)} %copy-done), custom_call_target="tpu_custom_call" | custom-call | tf_op jit(solution)/shard_map/reduce_parts/pallas_call | solution.py:348
  104.8 0.0 copy-start.7
  104.8 0.6 copy-done.7
  105.4 3.0 %means.1 = (f32[256,32]{1,0:T(8,128)}, f32[256,32]{1,0:T(8,128)}) custom-call(f32[4,5,8,128]{3,2,1,0:T(8,128)} %copy-done.7), custom_call_target="tpu_custom_call" | custom-call | tf_op jit(solution)/shard_map/means/pallas_call | solution.py:392
  108.5 1.6 %copy.8 = f32[256,32]{0,1:T(8,128)} copy(f32[256,32]{1,0:T(8,128)} %get-tuple-element.2) | data formatting | bytes 65536 | tf_op jit(solution)/shard_map/means/pallas_call | solution.py:392
  110.0 1.6 %copy.9 = f32[256,32]{0,1:T(8,128)} copy(f32[256,32]{1,0:T(8,128)} %get-tuple-element.3) | data formatting | bytes 65536 | tf_op jit(solution)/shard_map/means/pallas_call | solution.py:392
Async XLA Ops:
  0.6 1.0 copy-start.2
  1.6 0.9 copy-start.4
  2.5 1.2 %copy-start.6 = (s32[262144]{0:T(1024)S(1)}, s32[262144]{0:T(1024)}, u32[]{:S(2)}) copy-start(s32[262144]{0:T(1024)} %param.9) | copy-start | bytes 3145732
  3.8 0.7 copy-start.8
  29.8 1.2 %copy-start.1 = (bf16[512,1024]{1,0:T(8,128)(2,1)S(1)}, bf16[512,1024]{1,0:T(8,128)(2,1)}, u32[]{:S(2)}) copy-start(bf16[512,1024]{1,0:T(8,128)(2,1)} %vectors.1) | copy-start | bytes 3145732
  31.1 0.9 copy-start.3
  32.0 0.9 copy-start.5
  65.1 1.7 %copy-start = (f32[2,16,4,5,8,128]{5,4,3,2,1,0:T(8,128)S(1)}, f32[2,16,4,5,8,128]{5,4,3,2,1,0:T(8,128)}, u32[]{:S(2)}) copy-start(f32[2,16,4,5,8,128]{5,4,3,2,1,0:T(8,128)} %local_sums.1.parts) | copy-start | bytes 7864324
  104.8 0.6 copy-start.7

commit v2 on v0

v2 whole, which is shorter than its diff:
```python
import jax
import jax.numpy as jnp
from jax import lax
from jax.experimental import pallas as pl
from jax.experimental.pallas import tpu as pltpu
from jax.sharding import PartitionSpec as P

K = 256
D = 1024
S = 128
DEV = 128
CAP = 8
ROWS_DEV = 512
CENT_DEV = 2048
ASKED = DEV * CAP
CHUNK = 256
LAG = 3
MESH = pl.DeviceIdType.MESH
F32 = jnp.float32
BF16 = jnp.bfloat16
I32 = jnp.int32


def iota(shape, dim):
    return lax.broadcasted_iota(I32, shape, dim)


def nt(a, b):
    return lax.dot_general(a, b, (((1,), (1,)), ((), ())), preferred_element_type=F32)


def nn(a, b):
    return jnp.dot(a, b, preferred_element_type=F32)


def one_hot(match):
    return jnp.where(match, 1.0, 0.0).astype(BF16)


def narrow(whole):
    return whole.astype(F32).astype(BF16)


def kernel(
    ids,
    place_hbm,
    first_hbm,
    second_hbm,
    vectors_hbm,
    table_hbm,
    out_first,
    out_second,
    place,
    first,
    second,
    vectors,
    table,
    found,
    send,
    recv,
    spread_own,
    high_own,
    low_own,
    wanted,
    spread_asked,
    high_asked,
    low_asked,
    parts,
    mate,
    half,
    landed,
    means,
    load_sem,
    send_sem,
    recv_sem,
    core_send,
    core_recv,
    part_send,
    part_recv,
    last_send,
    last_recv,
):
    rows_at = lax.axis_index("rows")
    z = lax.axis_index("rep")
    me = rows_at * 4 + z
    core = lax.rem(rows_at, 2)
    y = lax.rem(rows_at // 2, 4)
    x = rows_at // 8
    barrier = pltpu.get_barrier_semaphore()

    loads = []
    for at, (source, target) in enumerate(
        (
            (place_hbm, place),
            (first_hbm, first),
            (second_hbm, second),
            (vectors_hbm, vectors),
            (table_hbm, table),
        )
    ):
        load = pltpu.make_async_copy(source, target, load_sem.at[at])
        load.start()
        loads.append(load)

    def greet(step, unused):
        other = lax.rem(me + step, DEV)
        pl.semaphore_signal(
            barrier, inc=1, device_id=(other // 4, lax.rem(other, 4)), device_id_type=MESH
        )
        return unused

    lax.fori_loop(1, DEV, greet, 0)

    loads[0].wait()
    lanes = iota((1, 128), 1)

    def find(block, unused):
        for step in range(8):
            row = block * 8 + step
            wish = ids[row]
            found[pl.ds(row, 1), :] = jnp.where(
                lanes == (wish & 127), place[pl.ds(wish >> 7, 1), :], 0
            )
        return unused

    lax.fori_loop(0, ROWS_DEV // 8, find, 0)

    places = found[...]
    ones8 = jnp.ones((8, 128), BF16)
    owner_row = nt(ones8, narrow(places >> 11))[0:1, :].astype(I32)
    slot_high = nt(ones8, narrow((places >> 7) & 15))[0:1, :]
    slot_low = nt(ones8, narrow(places & 127))[0:1, :]
    owner_is = iota((DEV, ROWS_DEV), 0) == owner_row
    owner_hot = one_hot(owner_is)
    earlier = one_hot(iota((ROWS_DEV, ROWS_DEV), 0) < iota((ROWS_DEV, ROWS_DEV), 1))
    before = nn(owner_hot, earlier)
    rank = jnp.sum(jnp.where(owner_is, before, 0.0), axis=0, keepdims=True).astype(I32)
    rank_is = iota((DEV, ROWS_DEV), 0) == rank
    slots_high = nt(owner_hot, jnp.where(rank_is, slot_high, 0.0).astype(BF16))
    slots_low = nt(owner_hot, jnp.where(rank_is, slot_low, 0.0).astype(BF16))
    slots = (slots_high * 128.0 + slots_low).astype(I32)
    position = owner_row * CAP + rank
    loads[1].wait()
    loads[2].wait()
    payload = jnp.concatenate([narrow(first[...] + 1), narrow(second[...] + 1)], axis=1)
    for block in range(4):
        move = one_hot(iota((256, ROWS_DEV), 0) + 256 * block == position)
        moved = nn(move, payload).astype(I32)
        codes = moved[:, 0:128] + moved[:, 128:256] * 65536
        send[32 * block : 32 * block + 32, 0:8, :] = codes.reshape(32, CAP, 128)
    send[:, 8:9, :] = slots.reshape(DEV, 1, 128)

    pl.semaphore_wait(barrier, DEV - 1)

    def push(step, unused):
        other = lax.rem(me + step, DEV)
        pltpu.make_async_remote_copy(
            src_ref=send.at[other],
            dst_ref=recv.at[step],
            send_sem=send_sem,
            recv_sem=recv_sem,
            device_id=(other // 4, lax.rem(other, 4)),
            device_id_type=MESH,
        ).start()
        return unused

    lax.fori_loop(1, DEV, push, 0)
    recv[0] = send[me]

    def lay_codes(column, high, low, index, start):
        turned = nt(eye128, narrow(column)) - 1.0
        low_part = jnp.floor(turned * (1.0 / 32.0))
        high[index, :, start : start + CHUNK] = turned - 32.0 * low_part
        low[index, :, start : start + CHUNK] = low_part

    eye128 = one_hot(iota((128, 128), 0) == iota((128, 128), 1))
    eye256 = one_hot(iota((256, 256), 0) == iota((256, 256), 1))

    high_is = narrow(iota((16, CHUNK), 0))
    count_is = narrow(iota((16, CHUNK), 0) & 7)
    wide_lane = iota((32, 256), 1)
    lane_sub = (wide_lane >> 7) * 2 + ((wide_lane >> 3) & 1)
    count_lane_sub = iota((32, 32), 1) >> 3
    one = jnp.ones((), BF16)
    zero = jnp.zeros((), BF16)

    def tally(spread, row, high, low, owner, chunks, index, counting):
        total = count = None
        for chunk in range(chunks):
            start = chunk * CHUNK
            left, right, mark = [], [], []
            for pair in range(2):
                data = spread[
                    pl.ds(pl.multiple_of(row + 16 * pair, 16), 16), start : start + CHUNK
                ]
                lows = []
                for sub in range(2):
                    at = owner * 4 + pair * 2 + sub
                    h = jnp.broadcast_to(high[index, pl.ds(at, 1), start : start + CHUNK], (8, CHUNK))
                    h = jnp.concatenate([h, h], axis=0).astype(BF16)
                    left.append(jnp.where(h == high_is, one, zero))
                    left.append(jnp.where(h == high_is + 16.0, one, zero))
                    lows.append(
                        jnp.broadcast_to(low[index, pl.ds(at, 1), start : start + CHUNK], (8, CHUNK))
                    )
                l = jnp.concatenate(lows, axis=0).astype(BF16)
                for value in range(8):
                    right.append(jnp.where(l == jnp.full((), value, BF16), data, zero))
                if counting:
                    mark.append(jnp.where(l == count_is, one, zero))
            left = jnp.concatenate(left, axis=0)
            product = nt(left, jnp.concatenate(right, axis=0))
            total = product if total is None else total + product
            if counting:
                product = nt(left, jnp.concatenate(mark, axis=0))
                count = product if count is None else count + product
        mine = total[0:32]
        mine_count = count[0:32] if counting else None
        for sub in range(1, 4):
            cut = slice(32 * sub, 32 * sub + 32)
            mine = jnp.where(lane_sub == sub, total[cut], mine)
            if counting:
                mine_count = jnp.where(count_lane_sub == sub, count[cut], mine_count)
        return mine, mine_count

    def spot_of(turn):
        x_to = lax.rem(x + turn // 4 + 1, 4)
        y_to = lax.rem(y + lax.rem(turn, 4) + 1, 4)
        return x_to * 4 + y_to

    loads[3].wait()
    for chunk in range(ROWS_DEV // CHUNK):
        start = chunk * CHUNK
        for block in range(D // 256):
            cut = vectors[start : start + CHUNK, block * 256 : (block + 1) * 256]
            spread_own[block * 256 : (block + 1) * 256, start : start + CHUNK] = nt(
                eye256, cut
            ).astype(BF16)
        lay_codes(first[start : start + CHUNK, :] + 1, high_own, low_own, 0, start)
        lay_codes(second[start : start + CHUNK, :] + 1, high_own, low_own, 1, start)

    def own_step(step, unused):
        turn, side = step // 2, lax.rem(step, 2)
        owner = spot_of(turn) * 2 + side
        counted = []
        for index in range(2):
            mine, count = tally(
                spread_own, owner * 32, high_own, low_own, owner, ROWS_DEV // CHUNK, index, True
            )
            parts[side, turn, :, 2 * index] = mine[:, 0:128].reshape(4, 8, 128)
            parts[side, turn, :, 2 * index + 1] = mine[:, 128:256].reshape(4, 8, 128)
            counted.append(count)
        counted.append(jnp.zeros((32, 64), F32))
        parts[side, turn, :, 4] = jnp.concatenate(counted, axis=1).reshape(4, 8, 128)
        return unused

    lax.fori_loop(0, 32, own_step, 0)

    rest = recv.at[pl.ds(1, DEV - 1)]
    pltpu.make_async_copy(rest, rest, recv_sem).wait()
    loads[4].wait()
    ones128 = jnp.ones((128, 128), BF16)
    slots_in = recv[:, 8:9, :].reshape(DEV, 128)
    slots_high = narrow(slots_in >> 7)
    slots_low = narrow(slots_in & 127)
    for chunk in range(ASKED // CHUNK):
        start = chunk * CHUNK
        codes = recv[32 * chunk : 32 * chunk + 32, 0:8, :].reshape(CHUNK, 128)
        lay_codes(codes & 65535, high_asked, low_asked, 0, start)
        lay_codes(codes >> 16, high_asked, low_asked, 1, start)
        row_at = iota((CHUNK, 128), 0)
        lane = iota((CHUNK, 128), 1)
        fan = one_hot((row_at >> 3) + 32 * chunk == lane)
        keep = (row_at & 7) == lane
        slot_high = nn(jnp.where(keep, nn(fan, slots_high), 0.0).astype(BF16), ones128).astype(BF16)
        slot_low = nn(jnp.where(keep, nn(fan, slots_low), 0.0).astype(BF16), ones128).astype(BF16)
        low_hot = jnp.where(slot_low == narrow(lane), one, zero)
        for block in range(CENT_DEV // 128):
            wanted[start : start + CHUNK, block * 128 : (block + 1) * 128] = jnp.where(
                slot_high == jnp.full((), block, BF16), low_hot, zero
            )

    mate_id = (rows_at + 1 - 2 * core, z)

    def core_copy(turn):
        return pltpu.make_async_remote_copy(
            src_ref=parts.at[1 - core, turn],
            dst_ref=mate.at[turn],
            send_sem=core_send.at[turn],
            recv_sem=core_recv.at[turn],
            device_id=mate_id,
            device_id_type=MESH,
        )

    def part_copy(turn, z_step):
        z_to = lax.rem(z + z_step, 4)
        return pltpu.make_async_remote_copy(
            src_ref=half.at[turn, z_to],
            dst_ref=landed.at[turn * 4 + 3 - z_step],
            send_sem=part_send,
            recv_sem=part_recv,
            device_id=(spot_of(turn) * 2 + core, z_to),
            device_id_type=MESH,
        )

    def pass_on(turn):
        core_copy(turn).wait_recv()
        half[turn] = parts[core, turn] + mate[turn]
        for z_step in range(1, 4):
            part_copy(turn, z_step).start()

        @pl.when(turn != 15)
        def _():
            part_copy(turn, 0).start()

    def block_step(block, unused):
        x_to = lax.rem(x + block + 1, 4)
        columns = pl.ds(pl.multiple_of(x_to * 256, 256), 256)
        base = nn(wanted[...], table[:, columns]).astype(BF16)
        for chunk in range(ASKED // CHUNK):
            start = chunk * CHUNK
            spread_asked[:, start : start + CHUNK] = nt(-eye256, base[start : start + CHUNK]).astype(
                BF16
            )

        def spot_step(spot, unused_too):
            turn = block * 4 + spot
            y_to = lax.rem(y + spot + 1, 4)

            def side_step(side, unused_three):
                owner = spot_of(turn) * 2 + side
                for index in range(2):
                    mine, unused_count = tally(
                        spread_asked,
                        (y_to * 2 + side) * 32,
                        high_asked,
                        low_asked,
                        owner,
                        ASKED // CHUNK,
                        index,
                        False,
                    )
                    parts[side, turn, :, 2 * index] += mine[:, 0:128].reshape(4, 8, 128)
                    parts[side, turn, :, 2 * index + 1] += mine[:, 128:256].reshape(4, 8, 128)
                return unused_three

            lax.fori_loop(0, 2, side_step, 0)
            core_copy(turn).start()

            @pl.when(turn >= LAG)
            def _():
                pass_on(turn - LAG)

            return unused_too

        lax.fori_loop(0, 4, spot_step, 0)
        return unused

    lax.fori_loop(0, 4, block_step, 0)
    for turn in range(16 - LAG, 16):
        pass_on(jnp.int32(turn))

    others = landed.at[pl.ds(0, 63)]
    pltpu.make_async_copy(others, others, part_recv).wait()

    def add(step, total):
        return total + landed[step]

    total = lax.fori_loop(0, 63, add, half[15, z])

    count = jnp.maximum(total[4], 1.0)
    count_high = jnp.floor(count * (1.0 / 256.0))
    count_low = (count - 256.0 * count_high).astype(BF16)
    count_high = count_high.astype(BF16)
    from_lane = iota((128, 256), 0)
    lane = iota((128, 256), 1)
    sub_lane = ((lane >> 7) * 2 + ((lane >> 3) & 1)) * 8 + ((lane >> 4) & 7)
    for index in range(2):
        fan = one_hot(from_lane == index * 32 + sub_lane)
        fanned = 256.0 * nn(count_high, fan) + nn(count_low, fan)
        means[z, 2 * index] = total[2 * index] / fanned[:, 0:128]
        means[z, 2 * index + 1] = total[2 * index + 1] / fanned[:, 128:256]

    for z_step in range(1, 4):
        pltpu.make_async_remote_copy(
            src_ref=means.at[z],
            dst_ref=means.at[z],
            send_sem=last_send,
            recv_sem=last_recv,
            device_id=(rows_at, lax.rem(z + z_step, 4)),
            device_id_type=MESH,
        ).start()
    three = means.at[pl.ds(0, 3)]
    pltpu.make_async_copy(three, three, last_recv).wait()
    for index, out in ((0, out_first), (1, out_second)):
        both = jnp.concatenate(
            [means[:, 2 * index].reshape(32, 128), means[:, 2 * index + 1].reshape(32, 128)], axis=1
        ).T
        out[...] = jnp.concatenate(
            [
                jnp.concatenate([both[16 * v : 16 * v + 16], both[128 + 16 * v : 144 + 16 * v]], axis=0)
                for v in range(8)
            ],
            axis=1,
        )

    pltpu.make_async_copy(three, three, last_send).wait()
    pltpu.make_async_copy(others, others, part_send).wait()
    pltpu.make_async_copy(rest, rest, send_sem).wait()

    def end_core(turn, unused):
        core_copy(turn).wait_send()
        return unused

    lax.fori_loop(0, 16, end_core, 0)


def on_device(vectors, list_ids, centroids, list_place, codes_first, codes_second):
    place = list_place.reshape(2048, 128)
    vmem, dma = pltpu.VMEM, pltpu.SemaphoreType.DMA
    first, second = pl.pallas_call(
        kernel,
        out_shape=[jax.ShapeDtypeStruct((32, K), F32)] * 2,
        in_specs=[pl.BlockSpec(memory_space=pltpu.SMEM)]
        + [pl.BlockSpec(memory_space=pl.ANY)] * 5,
        out_specs=[pl.BlockSpec(memory_space=pltpu.VMEM)] * 2,
        scratch_shapes=[
            vmem((2048, 128), I32),
            vmem((ROWS_DEV, S), I32),
            vmem((ROWS_DEV, S), I32),
            vmem((ROWS_DEV, D), BF16),
            vmem((CENT_DEV, D), BF16),
            vmem((ROWS_DEV, 128), I32),
            vmem((DEV, 9, 128), I32),
            vmem((DEV, 9, 128), I32),
            vmem((D, ROWS_DEV), BF16),
            vmem((2, S, ROWS_DEV), F32),
            vmem((2, S, ROWS_DEV), F32),
            vmem((ASKED, CENT_DEV), BF16),
            vmem((256, ASKED), BF16),
            vmem((2, S, ASKED), F32),
            vmem((2, S, ASKED), F32),
            vmem((2, 16, 4, 5, 8, 128), F32),
            vmem((16, 4, 5, 8, 128), F32),
            vmem((16, 4, 5, 8, 128), F32),
            vmem((63, 5, 8, 128), F32),
            vmem((4, 4, 8, 128), F32),
            dma((5,)),
            dma,
            dma,
            dma((16,)),
            dma((16,)),
            dma,
            dma,
            dma,
            dma,
        ],
        compiler_params=pltpu.CompilerParams(
            collective_id=0, has_side_effects=True, vmem_limit_bytes=60 * 2**20
        ),
        name="codebooks",
    )(list_ids, place, codes_first, codes_second, vectors, centroids)
    return (first.T, second.T)


def solution(mesh):
    return jax.shard_map(
        on_device,
        mesh=mesh,
        in_specs=(
            P(("rows", "rep"), None),
            P(("rows", "rep")),
            P(("rows", "rep"), None),
            P(),
            P(("rows", "rep"), None),
            P(("rows", "rep"), None),
        ),
        out_specs=(P(None, "rows"), P(None, "rows")),
        check_vma=False,
    )
```

time: 314 us -> 69.3 us (0.22)
  waiting for transfers between devices: 95.9 us -> 0 us
  other arithmetic: 66.5 us -> 0 us
  Pallas kernels: 0 us -> 65.6 us
  local copies, waits for them, and re-layouts: 49.5 us -> 2.75 us
  matrix products: 43.4 us -> 0 us
  blocking collectives: 20 us -> 0 us
  starting transfers between devices: 18.6 us -> 0 us
  between operations: 14.3 us -> 0.64 us
  loops' own time: 5.27 us -> 0 us
    pallas_call x0 -> x1, Pallas kernels: none -> 65.6 us  [on_device(): pl.pallas_call(kernel, out_shape=[jax.ShapeDtypeStruct((32, K), F32)] * 2...]
    all_to_all x4 -> x0, waiting for transfers between devices: 58.1 us -> none  [the longest x1 28.3 us: fetch_residual(): lax.all_to_all(answer, ('rows', 'rep'), split_axis=0, concat_axis=0, tile...]
    reduce_sum x5 -> x0, other arithmetic: 54.4 us -> none  [the longest x4 54.3 us: add_block(): block_counts = jnp.sum(one_hot, axis=0, dtype=jnp.float32)]
    dot_general x4 -> x0, matrix products: 43.4 us -> none  [add_block(): jnp.einsum('rsk,rsc->skc', one_hot, row_block, preferred_element_type=jnp...]
    psum x1 -> x0, waiting for transfers between devices: 37.8 us -> none  [finish(): lax.psum((first_sums, first_counts, second_sums, second_counts), 'rep')]
    gather x5 -> x0, local copies, waits for them, and re-layouts: 20.5 us -> none  [the longest x1 7.71 us: fetch_residual(): answer = jnp.take(centroids, wanted_ids.reshape(-1), axis=0)]
    all_to_all x1 -> x0, blocking collectives: 20 us -> none  [fetch_residual(): lax.all_to_all(request, ('rows', 'rep'), split_axis=0, concat_axis=0, til...]
    all_to_all x4 -> x0, starting transfers between devices: 18.4 us -> none  [the longest x1 5.01 us: on_device(): lax.all_to_all(residual, 'rows', split_axis=1, concat_axis=0, tiled=True)]
  transfers between devices with their start and end apart: 5 -> 0, of which waited for: 5 -> 0; matrix products, arithmetic and copies ran while one was open for 5% -> 0% of each run, Pallas kernels for 0% -> 0%
where the time goes in v2:
time: 69.3 us; the launch traced here: 69 us
  Pallas kernels  65.6 us (95%)
  local copies, waits for them, and re-layouts  2.75 us (4%)
    pallas_call x1, Pallas kernels, on_device(): pl.pallas_call(kernel, out_shape=[jax.ShapeDtypeStruct((32, K), F32)] * 2...  65.6 us
    unnamed x2, local copies, waits for them, and re-layouts  2.75 us

profile of v2, /device:TPU:0, one launch (start us, length us, event | category | flops | bytes accessed | tf_op | source)
XLA Modules:
  0.0 69.0 jit_solution(12539580756404948249)
XLA Ops:
  0.6 65.6 %codebooks.1 = (f32[32,256]{1,0:T(8,128)}, f32[32,256]{1,0:T(8,128)}) custom-call(s32[512]{0:T(512)} %ids.1, s32[2048,128]{1,0:T(8,128)} %bitcast.3, s32[512,128]{1,0:T(8,128)} %first_hbm.1, s32[512,128]{1,0:T(8,128)} %second_hbm.1, bf16[512,1024]{1,0:T(8,128)(2,1)} %vectors_hbm.1, bf16[2048,1024]{1,0:T(8,128)(2,1)} %table_hbm.1), custom_call_target="tpu_custom_call" | custom-call | tf_op jit(solution)/shard_map/codebooks/pallas_call | solution.py:421
  66.2 1.4 %copy.10 = f32[256,32]{0,1:T(8,128)} copy(f32[256,32]{0,1:T(8,128)} %bitcast.5) | data formatting | bytes 65536
  67.6 1.4 %copy.11 = f32[256,32]{0,1:T(8,128)} copy(f32[256,32]{0,1:T(8,128)} %bitcast.4) | data formatting | bytes 65536

commit v3 on v2

--- a/solution.py
+++ b/solution.py
@@ -14,7 +14,7 @@
 CENT_DEV = 2048
 ASKED = DEV * CAP
 CHUNK = 256
-LAG = 3
+LAG = 1
 MESH = pl.DeviceIdType.MESH
 F32 = jnp.float32
 BF16 = jnp.bfloat16
@@ -61,6 +61,8 @@
     spread_own,
     high_own,
     low_own,
+    inner_own,
+    outer_own,
     wanted,
     spread_asked,
     high_asked,
@@ -69,6 +71,10 @@
     mate,
     half,
     landed,
+    counts,
+    count_mate,
+    count_half,
+    count_landed,
     means,
     load_sem,
     send_sem,
@@ -77,6 +83,10 @@
     core_recv,
     part_send,
     part_recv,
+    swap_send,
+    swap_recv,
+    count_send,
+    count_recv,
     last_send,
     last_recv,
 ):
@@ -158,8 +168,8 @@
             src_ref=send.at[other],
             dst_ref=recv.at[step],
             send_sem=send_sem,
-            recv_sem=recv_sem,
-            device_id=(other // 4, lax.rem(other, 4)),
+            recv_sem=recv_sem.at[step >> 5],
+            device_id=(other >> 2, other & 3),
             device_id_type=MESH,
         ).start()
         return unused
@@ -170,25 +180,31 @@
     def lay_codes(column, high, low, index, start):
         turned = nt(eye128, narrow(column)) - 1.0
         low_part = jnp.floor(turned * (1.0 / 32.0))
-        high[index, :, start : start + CHUNK] = turned - 32.0 * low_part
+        high_part = turned - 32.0 * low_part
+        high[index, :, start : start + CHUNK] = high_part
         low[index, :, start : start + CHUNK] = low_part
+        return high_part, low_part
+
+    def lay_own(column, index, start):
+        high_part, low_part = lay_codes(column, high_own, low_own, index, start)
+        odd = jnp.where(high_part >= 16.0, 1.0, 0.0)
+        inner_own[index, :, start : start + CHUNK] = high_part - 16.0 * odd
+        outer_own[index, :, start : start + CHUNK] = low_part + 8.0 * odd
 
     eye128 = one_hot(iota((128, 128), 0) == iota((128, 128), 1))
     eye256 = one_hot(iota((256, 256), 0) == iota((256, 256), 1))
 
     high_is = narrow(iota((16, CHUNK), 0))
-    count_is = narrow(iota((16, CHUNK), 0) & 7)
     wide_lane = iota((32, 256), 1)
     lane_sub = (wide_lane >> 7) * 2 + ((wide_lane >> 3) & 1)
-    count_lane_sub = iota((32, 32), 1) >> 3
     one = jnp.ones((), BF16)
     zero = jnp.zeros((), BF16)
 
-    def tally(spread, row, high, low, owner, chunks, index, counting):
-        total = count = None
-        for chunk in range(chunks):
+    def tally(spread, row, high, low, owner, chunks, index):
+        total = None
+        for chunk in chunks:
             start = chunk * CHUNK
-            left, right, mark = [], [], []
+            left, right = [], []
             for pair in range(2):
                 data = spread[
                     pl.ds(pl.multiple_of(row + 16 * pair, 16), 16), start : start + CHUNK
@@ -206,22 +222,12 @@
                 l = jnp.concatenate(lows, axis=0).astype(BF16)
                 for value in range(8):
                     right.append(jnp.where(l == jnp.full((), value, BF16), data, zero))
-                if counting:
-                    mark.append(jnp.where(l == count_is, one, zero))
-            left = jnp.concatenate(left, axis=0)
-            product = nt(left, jnp.concatenate(right, axis=0))
+            product = nt(jnp.concatenate(left, axis=0), jnp.concatenate(right, axis=0))
             total = product if total is None else total + product
-            if counting:
-                product = nt(left, jnp.concatenate(mark, axis=0))
-                count = product if count is None else count + product
         mine = total[0:32]
-        mine_count = count[0:32] if counting else None
         for sub in range(1, 4):
-            cut = slice(32 * sub, 32 * sub + 32)
-            mine = jnp.where(lane_sub == sub, total[cut], mine)
-            if counting:
-                mine_count = jnp.where(count_lane_sub == sub, count[cut], mine_count)
-        return mine, mine_count
+            mine = jnp.where(lane_sub == sub, total[32 * sub : 32 * sub + 32], mine)
+        return mine
 
     def spot_of(turn):
         x_to = lax.rem(x + turn // 4 + 1, 4)
@@ -236,51 +242,146 @@
             spread_own[block * 256 : (block + 1) * 256, start : start + CHUNK] = nt(
                 eye256, cut
             ).astype(BF16)
-        lay_codes(first[start : start + CHUNK, :] + 1, high_own, low_own, 0, start)
-        lay_codes(second[start : start + CHUNK, :] + 1, high_own, low_own, 1, start)
-
-    def own_step(step, unused):
-        turn, side = step // 2, lax.rem(step, 2)
-        owner = spot_of(turn) * 2 + side
-        counted = []
-        for index in range(2):
-            mine, count = tally(
-                spread_own, owner * 32, high_own, low_own, owner, ROWS_DEV // CHUNK, index, True
-            )
-            parts[side, turn, :, 2 * index] = mine[:, 0:128].reshape(4, 8, 128)
-            parts[side, turn, :, 2 * index + 1] = mine[:, 128:256].reshape(4, 8, 128)
-            counted.append(count)
-        counted.append(jnp.zeros((32, 64), F32))
-        parts[side, turn, :, 4] = jnp.concatenate(counted, axis=1).reshape(4, 8, 128)
-        return unused
-
-    lax.fori_loop(0, 32, own_step, 0)
-
-    rest = recv.at[pl.ds(1, DEV - 1)]
-    pltpu.make_async_copy(rest, rest, recv_sem).wait()
+        lay_own(first[start : start + CHUNK, :] + 1, 0, start)
+        lay_own(second[start : start + CHUNK, :] + 1, 1, start)
+
+    def own_step(turn, unused):
+        for side in range(2):
+            owner = spot_of(turn) * 2 + side
+            for index in range(2):
+                mine = tally(
+                    spread_own, owner * 32, high_own, low_own, owner, range(ROWS_DEV // CHUNK), index
+                )
+                parts[side, turn, :, 2 * index] = mine[:, 0:128].reshape(4, 8, 128)
+                parts[side, turn, :, 2 * index + 1] = mine[:, 128:256].reshape(4, 8, 128)
+        return unused
+
+
+    sixteen = narrow(iota((16, CHUNK), 0))
+    count_lane = iota((16, 256), 1) >> 4
+
+    def count_step(turn, unused):
+        total = None
+        for chunk in range(ROWS_DEV // CHUNK):
+            start = chunk * CHUNK
+            left, right = [], []
+            for side in range(2):
+                for index in range(2):
+                    for sub in range(4):
+                        at = pl.ds((spot_of(turn) * 2 + side) * 4 + sub, 1)
+                        for source, target in ((inner_own, left), (outer_own, right)):
+                            code = jnp.broadcast_to(
+                                source[index, at, start : start + CHUNK], (8, CHUNK)
+                            )
+                            code = jnp.concatenate([code, code], axis=0).astype(BF16)
+                            target.append(jnp.where(code == sixteen, one, zero))
+            product = nt(jnp.concatenate(left, axis=0), jnp.concatenate(right, axis=0))
+            total = product if total is None else total + product
+        mine = total[0:16]
+        for at in range(1, 16):
+            mine = jnp.where(count_lane == at, total[16 * at : 16 * at + 16], mine)
+        for side in range(2):
+            counts[side, turn] = mine[:, 128 * side : 128 * side + 128].reshape(2, 8, 128)
+        return unused
+
+    lax.fori_loop(0, 16, count_step, 0)
+
+    mate_id = (rows_at + 1 - 2 * core, z)
+    count_swap = pltpu.make_async_remote_copy(
+        src_ref=counts.at[1 - core],
+        dst_ref=count_mate,
+        send_sem=swap_send,
+        recv_sem=swap_recv,
+        device_id=mate_id,
+        device_id_type=MESH,
+    )
+    count_swap.start()
+    lax.fori_loop(0, 16, own_step, 0)
+
+    def count_copy(turn, z_step):
+        z_to = lax.rem(z + z_step, 4)
+        return pltpu.make_async_remote_copy(
+            src_ref=count_half.at[turn, lax.rem(z_to, 2)],
+            dst_ref=count_landed.at[turn * 4 + 3 - z_step],
+            send_sem=count_send,
+            recv_sem=count_recv,
+            device_id=(spot_of(turn) * 2 + core, z_to),
+            device_id_type=MESH,
+        )
+
+    def send_counts(step, unused):
+        turn = step // 4
+        count_copy(turn, 3 - lax.rem(step, 4)).start()
+        return unused
+
     loads[4].wait()
     ones128 = jnp.ones((128, 128), BF16)
-    slots_in = recv[:, 8:9, :].reshape(DEV, 128)
-    slots_high = narrow(slots_in >> 7)
-    slots_low = narrow(slots_in & 127)
-    for chunk in range(ASKED // CHUNK):
+
+    def lay_asked(chunk):
+        arrived = recv.at[pl.ds(max(32 * chunk, 1), 32 if chunk else 31)]
+        pltpu.make_async_copy(arrived, arrived, recv_sem.at[chunk]).wait()
         start = chunk * CHUNK
         codes = recv[32 * chunk : 32 * chunk + 32, 0:8, :].reshape(CHUNK, 128)
         lay_codes(codes & 65535, high_asked, low_asked, 0, start)
         lay_codes(codes >> 16, high_asked, low_asked, 1, start)
+        slots_in = recv[32 * chunk : 32 * chunk + 32, 8:9, :].reshape(32, 128)
         row_at = iota((CHUNK, 128), 0)
         lane = iota((CHUNK, 128), 1)
-        fan = one_hot((row_at >> 3) + 32 * chunk == lane)
+        fan = one_hot((iota((CHUNK, 32), 0) >> 3) == iota((CHUNK, 32), 1))
         keep = (row_at & 7) == lane
-        slot_high = nn(jnp.where(keep, nn(fan, slots_high), 0.0).astype(BF16), ones128).astype(BF16)
-        slot_low = nn(jnp.where(keep, nn(fan, slots_low), 0.0).astype(BF16), ones128).astype(BF16)
+        slot_high = nn(fan, narrow(slots_in >> 7))
+        slot_low = nn(fan, narrow(slots_in & 127))
+        slot_high = nn(jnp.where(keep, slot_high, 0.0).astype(BF16), ones128).astype(BF16)
+        slot_low = nn(jnp.where(keep, slot_low, 0.0).astype(BF16), ones128).astype(BF16)
         low_hot = jnp.where(slot_low == narrow(lane), one, zero)
         for block in range(CENT_DEV // 128):
             wanted[start : start + CHUNK, block * 128 : (block + 1) * 128] = jnp.where(
                 slot_high == jnp.full((), block, BF16), low_hot, zero
             )
 
-    mate_id = (rows_at + 1 - 2 * core, z)
+    def fetch(block, low_chunk, high_chunk):
+        x_to = lax.rem(x + block + 1, 4)
+        columns = pl.ds(pl.multiple_of(x_to * 256, 256), 256)
+        base = nn(
+            wanted[low_chunk * CHUNK : high_chunk * CHUNK, :], table[:, columns]
+        ).astype(BF16)
+        for chunk in range(low_chunk, high_chunk):
+            at = (chunk - low_chunk) * CHUNK
+            spread_asked[:, chunk * CHUNK : (chunk + 1) * CHUNK] = nt(
+                -eye256, base[at : at + CHUNK]
+            ).astype(BF16)
+
+    def add_asked(turn, side, low_chunk, high_chunk):
+        spot = spot_of(turn)
+        for index in range(2):
+            mine = tally(
+                spread_asked,
+                (lax.rem(spot, 4) * 2 + side) * 32,
+                high_asked,
+                low_asked,
+                spot * 2 + side,
+                range(low_chunk, high_chunk),
+                index,
+            )
+            parts[side, turn, :, 2 * index] += mine[:, 0:128].reshape(4, 8, 128)
+            parts[side, turn, :, 2 * index + 1] += mine[:, 128:256].reshape(4, 8, 128)
+
+    def early_block(block, unused):
+        fetch(block, 0, 1)
+
+        def early_step(step, unused_too):
+            for side in range(2):
+                add_asked(block * 4 + step, side, 0, 1)
+            return unused_too
+
+        lax.fori_loop(0, 4, early_step, 0)
+        return unused
+
+    for chunk in range(ASKED // CHUNK):
+        lay_asked(chunk)
+    count_swap.wait_recv()
+    count_half[...] = counts[core] + count_mate[...]
+    lax.fori_loop(0, 63, send_counts, 0)
 
     def core_copy(turn):
         return pltpu.make_async_remote_copy(
@@ -314,37 +415,13 @@
             part_copy(turn, 0).start()
 
     def block_step(block, unused):
-        x_to = lax.rem(x + block + 1, 4)
-        columns = pl.ds(pl.multiple_of(x_to * 256, 256), 256)
-        base = nn(wanted[...], table[:, columns]).astype(BF16)
-        for chunk in range(ASKED // CHUNK):
-            start = chunk * CHUNK
-            spread_asked[:, start : start + CHUNK] = nt(-eye256, base[start : start + CHUNK]).astype(
-                BF16
-            )
+        fetch(block, 0, ASKED // CHUNK)
 
         def spot_step(spot, unused_too):
             turn = block * 4 + spot
-            y_to = lax.rem(y + spot + 1, 4)
-
-            def side_step(side, unused_three):
-                owner = spot_of(turn) * 2 + side
-                for index in range(2):
-                    mine, unused_count = tally(
-                        spread_asked,
-                        (y_to * 2 + side) * 32,
-                        high_asked,
-                        low_asked,
-                        owner,
-                        ASKED // CHUNK,
-                        index,
-                        False,
-                    )
-                    parts[side, turn, :, 2 * index] += mine[:, 0:128].reshape(4, 8, 128)
-                    parts[side, turn, :, 2 * index + 1] += mine[:, 128:256].reshape(4, 8, 128)
-                return unused_three
-
-            lax.fori_loop(0, 2, side_step, 0)
+
+            for side in range(2):
+                add_asked(turn, side, 0, ASKED // CHUNK)
             core_copy(turn).start()
 
             @pl.when(turn >= LAG)
@@ -367,16 +444,21 @@
         return total + landed[step]
 
     total = lax.fori_loop(0, 63, add, half[15, z])
-
-    count = jnp.maximum(total[4], 1.0)
+    pltpu.make_async_copy(count_landed, count_landed, count_recv).wait()
+
+    def add_count(step, total):
+        return total + count_landed[step]
+
+    count = lax.fori_loop(0, 63, add_count, count_half[15, lax.rem(z, 2)])
+    count = jnp.maximum(count, 1.0)
     count_high = jnp.floor(count * (1.0 / 256.0))
     count_low = (count - 256.0 * count_high).astype(BF16)
     count_high = count_high.astype(BF16)
     from_lane = iota((128, 256), 0)
     lane = iota((128, 256), 1)
-    sub_lane = ((lane >> 7) * 2 + ((lane >> 3) & 1)) * 8 + ((lane >> 4) & 7)
+    sub_lane = ((lane >> 7) * 2 + ((lane >> 3) & 1)) * 16 + (z // 2) * 8 + ((lane >> 4) & 7)
     for index in range(2):
-        fan = one_hot(from_lane == index * 32 + sub_lane)
+        fan = one_hot(from_lane == index * 64 + sub_lane)
         fanned = 256.0 * nn(count_high, fan) + nn(count_low, fan)
         means[z, 2 * index] = total[2 * index] / fanned[:, 0:128]
         means[z, 2 * index + 1] = total[2 * index + 1] / fanned[:, 128:256]
@@ -406,6 +488,9 @@
 
     pltpu.make_async_copy(three, three, last_send).wait()
     pltpu.make_async_copy(others, others, part_send).wait()
+    pltpu.make_async_copy(count_landed, count_landed, count_send).wait()
+    count_swap.wait_send()
+    rest = send.at[pl.ds(1, DEV - 1)]
     pltpu.make_async_copy(rest, rest, send_sem).wait()
 
     def end_core(turn, unused):
@@ -413,6 +498,11 @@
         return unused
 
     lax.fori_loop(0, 16, end_core, 0)
+
+
+def hand_on(first, second, out_first, out_second):
+    out_first[...] = first[...]
+    out_second[...] = second[...]
 
 
 def on_device(vectors, list_ids, centroids, list_place, codes_first, codes_second):
@@ -436,20 +526,30 @@
             vmem((D, ROWS_DEV), BF16),
             vmem((2, S, ROWS_DEV), F32),
             vmem((2, S, ROWS_DEV), F32),
+            vmem((2, S, ROWS_DEV), F32),
+            vmem((2, S, ROWS_DEV), F32),
             vmem((ASKED, CENT_DEV), BF16),
             vmem((256, ASKED), BF16),
             vmem((2, S, ASKED), F32),
             vmem((2, S, ASKED), F32),
-            vmem((2, 16, 4, 5, 8, 128), F32),
-            vmem((16, 4, 5, 8, 128), F32),
-            vmem((16, 4, 5, 8, 128), F32),
-            vmem((63, 5, 8, 128), F32),
+            vmem((2, 16, 4, 4, 8, 128), F32),
+            vmem((16, 4, 4, 8, 128), F32),
+            vmem((16, 4, 4, 8, 128), F32),
+            vmem((63, 4, 8, 128), F32),
+            vmem((2, 16, 2, 8, 128), F32),
+            vmem((16, 2, 8, 128), F32),
+            vmem((16, 2, 8, 128), F32),
+            vmem((63, 8, 128), F32),
             vmem((4, 4, 8, 128), F32),
             dma((5,)),
             dma,
-            dma,
+            dma((4,)),
             dma((16,)),
             dma((16,)),
+            dma,
+            dma,
+            dma,
+            dma,
             dma,
             dma,
             dma,
@@ -460,6 +560,13 @@
         ),
         name="codebooks",
     )(list_ids, place, codes_first, codes_second, vectors, centroids)
+    first, second = pl.pallas_call(
+        hand_on,
+        out_shape=[jax.ShapeDtypeStruct((32, K), F32)] * 2,
+        in_specs=[pl.BlockSpec(memory_space=vmem)] * 2,
+        out_specs=[pl.BlockSpec(memory_space=vmem)] * 2,
+        name="hand_on",
+    )(first, second)
     return (first.T, second.T)
 
 

time: 69.3 us -> 64.8 us (0.935)
  local copies, waits for them, and re-layouts: 2.75 us -> 0 us
  Pallas kernels: 65.6 us -> 63.5 us
    pallas_call x1, Pallas kernels: 65.6 us -> 62.1 us  [on_device(): pl.pallas_call(kernel, out_shape=[jax.ShapeDtypeStruct((32, K), F32)] * 2...]
    unnamed x2 -> x0, local copies, waits for them, and re-layouts: 2.75 us -> none
    pallas_call x0 -> x1, Pallas kernels: none -> 1.4 us  [on_device(): pl.pallas_call(hand_on, out_shape=[jax.ShapeDtypeStruct((32, K), F32)] *...]
where the time goes in v3:
time: 64.8 us; the launch traced here: 64.2 us
  Pallas kernels  63.5 us (98%)
    pallas_call x1, Pallas kernels, on_device(): pl.pallas_call(kernel, out_shape=[jax.ShapeDtypeStruct((32, K), F32)] * 2...  62.1 us
    pallas_call x1, Pallas kernels, on_device(): pl.pallas_call(hand_on, out_shape=[jax.ShapeDtypeStruct((32, K), F32)] *...  1.4 us

profile of v3, /device:TPU:0, one launch (start us, length us, event | category | flops | bytes accessed | tf_op | source)
XLA Modules:
  0.0 64.2 jit_solution(8924182403421831557)
XLA Ops:
  0.6 62.1 %codebooks.1 = (f32[32,256]{1,0:T(8,128)}, f32[32,256]{1,0:T(8,128)}) custom-call(s32[512]{0:T(512)} %ids.1, s32[2048,128]{1,0:T(8,128)} %bitcast.3, s32[512,128]{1,0:T(8,128)} %first_hbm.1, s32[512,128]{1,0:T(8,128)} %second_hbm.1, bf16[512,1024]{1,0:T(8,128)(2,1)} %vectors_hbm.1, bf16[2048,1024]{1,0:T(8,128)(2,1)} %table_hbm.1), custom_call_target="tpu_custom_call" | custom-call | tf_op jit(solution)/shard_map/codebooks/pallas_call | solution.py:511
  62.7 1.4 %hand_on.1 = (f32[32,256]{1,0:T(8,128)}, f32[32,256]{1,0:T(8,128)}) custom-call(f32[32,256]{1,0:T(8,128)} %get-tuple-element.6.first, f32[32,256]{1,0:T(8,128)} %get-tuple-element.7.second), custom_call_target="tpu_custom_call" | custom-call | tf_op jit(solution)/shard_map/hand_on/pallas_call | solution.py:563

commit v4 on v3

--- a/solution.py
+++ b/solution.py
@@ -42,7 +42,7 @@
 
 
 def kernel(
-    ids,
+    ids_hbm,
     place_hbm,
     first_hbm,
     second_hbm,
@@ -50,6 +50,7 @@
     table_hbm,
     out_first,
     out_second,
+    ids,
     place,
     first,
     second,
@@ -61,8 +62,6 @@
     spread_own,
     high_own,
     low_own,
-    inner_own,
-    outer_own,
     wanted,
     spread_asked,
     high_asked,
@@ -106,11 +105,13 @@
             (second_hbm, second),
             (vectors_hbm, vectors),
             (table_hbm, table),
+            (ids_hbm, ids),
         )
     ):
         load = pltpu.make_async_copy(source, target, load_sem.at[at])
-        load.start()
         loads.append(load)
+    for at in (5, 0, 1, 2):
+        loads[at].start()
 
     def greet(step, unused):
         other = lax.rem(me + step, DEV)
@@ -121,7 +122,10 @@
 
     lax.fori_loop(1, DEV, greet, 0)
 
+    loads[5].wait()
     loads[0].wait()
+    loads[3].start()
+    loads[4].start()
     lanes = iota((1, 128), 1)
 
     def find(block, unused):
@@ -183,28 +187,21 @@
         high_part = turned - 32.0 * low_part
         high[index, :, start : start + CHUNK] = high_part
         low[index, :, start : start + CHUNK] = low_part
-        return high_part, low_part
-
-    def lay_own(column, index, start):
-        high_part, low_part = lay_codes(column, high_own, low_own, index, start)
-        odd = jnp.where(high_part >= 16.0, 1.0, 0.0)
-        inner_own[index, :, start : start + CHUNK] = high_part - 16.0 * odd
-        outer_own[index, :, start : start + CHUNK] = low_part + 8.0 * odd
 
     eye128 = one_hot(iota((128, 128), 0) == iota((128, 128), 1))
     eye256 = one_hot(iota((256, 256), 0) == iota((256, 256), 1))
 
     high_is = narrow(iota((16, CHUNK), 0))
-    wide_lane = iota((32, 256), 1)
-    lane_sub = (wide_lane >> 7) * 2 + ((wide_lane >> 3) & 1)
+    lane_sub = iota((8, 128), 1) >> 5
+    count_is = narrow(iota((16, CHUNK), 0) & 7)
     one = jnp.ones((), BF16)
     zero = jnp.zeros((), BF16)
 
-    def tally(spread, row, high, low, owner, chunks, index):
+    def tally(spread, row, high, low, owner, chunks, index, counting):
         total = None
         for chunk in chunks:
             start = chunk * CHUNK
-            left, right = [], []
+            left, right, mark = [], [], []
             for pair in range(2):
                 data = spread[
                     pl.ds(pl.multiple_of(row + 16 * pair, 16), 16), start : start + CHUNK
@@ -222,12 +219,19 @@
                 l = jnp.concatenate(lows, axis=0).astype(BF16)
                 for value in range(8):
                     right.append(jnp.where(l == jnp.full((), value, BF16), data, zero))
-            product = nt(jnp.concatenate(left, axis=0), jnp.concatenate(right, axis=0))
+                if counting:
+                    mark.append(jnp.where(l == count_is, one, zero))
+            product = nt(jnp.concatenate(right + mark, axis=0), jnp.concatenate(left, axis=0))
             total = product if total is None else total + product
-        mine = total[0:32]
-        for sub in range(1, 4):
-            mine = jnp.where(lane_sub == sub, total[32 * sub : 32 * sub + 32], mine)
-        return mine
+
+        def own_lanes(rows):
+            mine = total[rows[0] : rows[0] + 8]
+            for sub in range(1, 4):
+                mine = jnp.where(lane_sub == sub, total[rows[sub] : rows[sub] + 8], mine)
+            return mine
+
+        sums = [own_lanes([16 * v, 16 * v + 8, 128 + 16 * v, 136 + 16 * v]) for v in range(8)]
+        return sums, own_lanes([256, 264, 272, 280]) if counting else None
 
     def spot_of(turn):
         x_to = lax.rem(x + turn // 4 + 1, 4)
@@ -242,49 +246,31 @@
             spread_own[block * 256 : (block + 1) * 256, start : start + CHUNK] = nt(
                 eye256, cut
             ).astype(BF16)
-        lay_own(first[start : start + CHUNK, :] + 1, 0, start)
-        lay_own(second[start : start + CHUNK, :] + 1, 1, start)
+        lay_codes(first[start : start + CHUNK, :] + 1, high_own, low_own, 0, start)
+        lay_codes(second[start : start + CHUNK, :] + 1, high_own, low_own, 1, start)
 
     def own_step(turn, unused):
         for side in range(2):
             owner = spot_of(turn) * 2 + side
             for index in range(2):
-                mine = tally(
-                    spread_own, owner * 32, high_own, low_own, owner, range(ROWS_DEV // CHUNK), index
+                sums, count = tally(
+                    spread_own,
+                    owner * 32,
+                    high_own,
+                    low_own,
+                    owner,
+                    range(ROWS_DEV // CHUNK),
+                    index,
+                    True,
                 )
-                parts[side, turn, :, 2 * index] = mine[:, 0:128].reshape(4, 8, 128)
-                parts[side, turn, :, 2 * index + 1] = mine[:, 128:256].reshape(4, 8, 128)
-        return unused
-
-
-    sixteen = narrow(iota((16, CHUNK), 0))
-    count_lane = iota((16, 256), 1) >> 4
-
-    def count_step(turn, unused):
-        total = None
-        for chunk in range(ROWS_DEV // CHUNK):
-            start = chunk * CHUNK
-            left, right = [], []
-            for side in range(2):
-                for index in range(2):
-                    for sub in range(4):
-                        at = pl.ds((spot_of(turn) * 2 + side) * 4 + sub, 1)
-                        for source, target in ((inner_own, left), (outer_own, right)):
-                            code = jnp.broadcast_to(
-                                source[index, at, start : start + CHUNK], (8, CHUNK)
-                            )
-                            code = jnp.concatenate([code, code], axis=0).astype(BF16)
-                            target.append(jnp.where(code == sixteen, one, zero))
-            product = nt(jnp.concatenate(left, axis=0), jnp.concatenate(right, axis=0))
-            total = product if total is None else total + product
-        mine = total[0:16]
-        for at in range(1, 16):
-            mine = jnp.where(count_lane == at, total[16 * at : 16 * at + 16], mine)
-        for side in range(2):
-            counts[side, turn] = mine[:, 128 * side : 128 * side + 128].reshape(2, 8, 128)
-        return unused
-
-    lax.fori_loop(0, 16, count_step, 0)
+                for value in range(8):
+                    z_of, at = value // 2, 2 * index + value % 2
+                    parts[side, turn, z_of, at] = sums[value]
+                    counts[side, turn, z_of, at : at + 1, :] = count[value : value + 1]
+        return unused
+
+
+    lax.fori_loop(0, 16, own_step, 0)
 
     mate_id = (rows_at + 1 - 2 * core, z)
     count_swap = pltpu.make_async_remote_copy(
@@ -296,12 +282,11 @@
         device_id_type=MESH,
     )
     count_swap.start()
-    lax.fori_loop(0, 16, own_step, 0)
 
     def count_copy(turn, z_step):
         z_to = lax.rem(z + z_step, 4)
         return pltpu.make_async_remote_copy(
-            src_ref=count_half.at[turn, lax.rem(z_to, 2)],
+            src_ref=count_half.at[turn, z_to],
             dst_ref=count_landed.at[turn * 4 + 3 - z_step],
             send_sem=count_send,
             recv_sem=count_recv,
@@ -354,7 +339,7 @@
     def add_asked(turn, side, low_chunk, high_chunk):
         spot = spot_of(turn)
         for index in range(2):
-            mine = tally(
+            sums, unused_count = tally(
                 spread_asked,
                 (lax.rem(spot, 4) * 2 + side) * 32,
                 high_asked,
@@ -362,9 +347,10 @@
                 spot * 2 + side,
                 range(low_chunk, high_chunk),
                 index,
+                False,
             )
-            parts[side, turn, :, 2 * index] += mine[:, 0:128].reshape(4, 8, 128)
-            parts[side, turn, :, 2 * index + 1] += mine[:, 128:256].reshape(4, 8, 128)
+            for value in range(8):
+                parts[side, turn, value // 2, 2 * index + value % 2] += sums[value]
 
     def early_block(block, unused):
         fetch(block, 0, 1)
@@ -379,9 +365,6 @@
 
     for chunk in range(ASKED // CHUNK):
         lay_asked(chunk)
-    count_swap.wait_recv()
-    count_half[...] = counts[core] + count_mate[...]
-    lax.fori_loop(0, 63, send_counts, 0)
 
     def core_copy(turn):
         return pltpu.make_async_remote_copy(
@@ -417,6 +400,13 @@
     def block_step(block, unused):
         fetch(block, 0, ASKED // CHUNK)
 
+        @pl.when(block == 1)
+        def _():
+            count_swap.wait_recv()
+            count_half[...] = counts[core] + count_mate[...]
+            lax.fori_loop(0, 63, send_counts, 0)
+
+
         def spot_step(spot, unused_too):
             turn = block * 4 + spot
 
@@ -449,19 +439,10 @@
     def add_count(step, total):
         return total + count_landed[step]
 
-    count = lax.fori_loop(0, 63, add_count, count_half[15, lax.rem(z, 2)])
+    count = lax.fori_loop(0, 63, add_count, count_half[15, z])
     count = jnp.maximum(count, 1.0)
-    count_high = jnp.floor(count * (1.0 / 256.0))
-    count_low = (count - 256.0 * count_high).astype(BF16)
-    count_high = count_high.astype(BF16)
-    from_lane = iota((128, 256), 0)
-    lane = iota((128, 256), 1)
-    sub_lane = ((lane >> 7) * 2 + ((lane >> 3) & 1)) * 16 + (z // 2) * 8 + ((lane >> 4) & 7)
-    for index in range(2):
-        fan = one_hot(from_lane == index * 64 + sub_lane)
-        fanned = 256.0 * nn(count_high, fan) + nn(count_low, fan)
-        means[z, 2 * index] = total[2 * index] / fanned[:, 0:128]
-        means[z, 2 * index + 1] = total[2 * index + 1] / fanned[:, 128:256]
+    for at in range(4):
+        means[z, at] = total[at] / count[at : at + 1, :]
 
     for z_step in range(1, 4):
         pltpu.make_async_remote_copy(
@@ -475,16 +456,14 @@
     three = means.at[pl.ds(0, 3)]
     pltpu.make_async_copy(three, three, last_recv).wait()
     for index, out in ((0, out_first), (1, out_second)):
-        both = jnp.concatenate(
-            [means[:, 2 * index].reshape(32, 128), means[:, 2 * index + 1].reshape(32, 128)], axis=1
-        ).T
-        out[...] = jnp.concatenate(
-            [
-                jnp.concatenate([both[16 * v : 16 * v + 16], both[128 + 16 * v : 144 + 16 * v]], axis=0)
-                for v in range(8)
-            ],
-            axis=1,
-        )
+        for sub in range(4):
+            out[8 * sub : 8 * sub + 8, :] = jnp.concatenate(
+                [
+                    means[v // 2, 2 * index + v % 2][:, 32 * sub : 32 * sub + 32]
+                    for v in range(8)
+                ],
+                axis=1,
+            )
 
     pltpu.make_async_copy(three, three, last_send).wait()
     pltpu.make_async_copy(others, others, part_send).wait()
@@ -511,10 +490,10 @@
     first, second = pl.pallas_call(
         kernel,
         out_shape=[jax.ShapeDtypeStruct((32, K), F32)] * 2,
-        in_specs=[pl.BlockSpec(memory_space=pltpu.SMEM)]
-        + [pl.BlockSpec(memory_space=pl.ANY)] * 5,
+        in_specs=[pl.BlockSpec(memory_space=pl.ANY)] * 6,
         out_specs=[pl.BlockSpec(memory_space=pltpu.VMEM)] * 2,
         scratch_shapes=[
+            pltpu.SMEM((ROWS_DEV,), I32),
             vmem((2048, 128), I32),
             vmem((ROWS_DEV, S), I32),
             vmem((ROWS_DEV, S), I32),
@@ -526,8 +505,6 @@
             vmem((D, ROWS_DEV), BF16),
             vmem((2, S, ROWS_DEV), F32),
             vmem((2, S, ROWS_DEV), F32),
-            vmem((2, S, ROWS_DEV), F32),
-            vmem((2, S, ROWS_DEV), F32),
             vmem((ASKED, CENT_DEV), BF16),
             vmem((256, ASKED), BF16),
             vmem((2, S, ASKED), F32),
@@ -536,12 +513,12 @@
             vmem((16, 4, 4, 8, 128), F32),
             vmem((16, 4, 4, 8, 128), F32),
             vmem((63, 4, 8, 128), F32),
-            vmem((2, 16, 2, 8, 128), F32),
-            vmem((16, 2, 8, 128), F32),
-            vmem((16, 2, 8, 128), F32),
-            vmem((63, 8, 128), F32),
+            vmem((2, 16, 4, 4, 128), F32),
+            vmem((16, 4, 4, 128), F32),
+            vmem((16, 4, 4, 128), F32),
+            vmem((63, 4, 128), F32),
             vmem((4, 4, 8, 128), F32),
-            dma((5,)),
+            dma((6,)),
             dma,
             dma((4,)),
             dma((16,)),

time: 64.8 us -> 58.4 us (0.901)
  Pallas kernels: 63.5 us -> 57.5 us
    pallas_call x1, Pallas kernels: 62.1 us -> 56.1 us  [on_device(): pl.pallas_call(kernel, out_shape=[jax.ShapeDtypeStruct((32, K), F32)] * 2...]
where the time goes in v4:
time: 58.4 us; the launch traced here: 58.2 us
  Pallas kernels  57.5 us (98%)
  between operations  0.64 us (1%)
    pallas_call x1, Pallas kernels, on_device(): pl.pallas_call(kernel, out_shape=[jax.ShapeDtypeStruct((32, K), F32)] * 2...  56.1 us
    pallas_call x1, Pallas kernels, on_device(): pl.pallas_call(hand_on, out_shape=[jax.ShapeDtypeStruct((32, K), F32)] *...  1.4 us

profile of v4, /device:TPU:0, one launch (start us, length us, event | category | flops | bytes accessed | tf_op | source)
XLA Modules:
  0.0 58.2 jit_solution(13353764828774200415)
XLA Ops:
  0.6 56.1 %codebooks.1 = (f32[32,256]{1,0:T(8,128)}, f32[32,256]{1,0:T(8,128)}) custom-call(s32[512]{0:T(512)} %ids_hbm.1, s32[2048,128]{1,0:T(8,128)} %bitcast.3, s32[512,128]{1,0:T(8,128)} %first_hbm.1, s32[512,128]{1,0:T(8,128)} %second_hbm.1, bf16[512,1024]{1,0:T(8,128)(2,1)} %vectors_hbm.1, bf16[2048,1024]{1,0:T(8,128)(2,1)} %table_hbm.1), custom_call_target="tpu_custom_call" | custom-call | tf_op jit(solution)/shard_map/codebooks/pallas_call | solution.py:490
  56.8 1.4 %hand_on.1 = (f32[32,256]{1,0:T(8,128)}, f32[32,256]{1,0:T(8,128)}) custom-call(f32[32,256]{1,0:T(8,128)} %get-tuple-element.6.first, f32[32,256]{1,0:T(8,128)} %get-tuple-element.7.second), custom_call_target="tpu_custom_call" | custom-call | tf_op jit(solution)/shard_map/hand_on/pallas_call | solution.py:540

commit v5 on v4

--- a/solution.py
+++ b/solution.py
@@ -14,7 +14,9 @@
 CENT_DEV = 2048
 ASKED = DEV * CAP
 CHUNK = 256
-LAG = 1
+WIDE = 512
+LAG = 2
+SPLIT = 12
 MESH = pl.DeviceIdType.MESH
 F32 = jnp.float32
 BF16 = jnp.bfloat16
@@ -57,6 +59,7 @@
     vectors,
     table,
     found,
+    earlier,
     send,
     recv,
     spread_own,
@@ -122,6 +125,8 @@
 
     lax.fori_loop(1, DEV, greet, 0)
 
+    earlier[...] = one_hot(iota((ROWS_DEV, ROWS_DEV), 0) < iota((ROWS_DEV, ROWS_DEV), 1))
+
     loads[5].wait()
     loads[0].wait()
     loads[3].start()
@@ -146,8 +151,7 @@
     slot_low = nt(ones8, narrow(places & 127))[0:1, :]
     owner_is = iota((DEV, ROWS_DEV), 0) == owner_row
     owner_hot = one_hot(owner_is)
-    earlier = one_hot(iota((ROWS_DEV, ROWS_DEV), 0) < iota((ROWS_DEV, ROWS_DEV), 1))
-    before = nn(owner_hot, earlier)
+    before = nn(owner_hot, earlier[...])
     rank = jnp.sum(jnp.where(owner_is, before, 0.0), axis=0, keepdims=True).astype(I32)
     rank_is = iota((DEV, ROWS_DEV), 0) == rank
     slots_high = nt(owner_hot, jnp.where(rank_is, slot_high, 0.0).astype(BF16))
@@ -191,30 +195,30 @@
     eye128 = one_hot(iota((128, 128), 0) == iota((128, 128), 1))
     eye256 = one_hot(iota((256, 256), 0) == iota((256, 256), 1))
 
-    high_is = narrow(iota((16, CHUNK), 0))
+    high_is = narrow(iota((16, WIDE), 0))
     lane_sub = iota((8, 128), 1) >> 5
-    count_is = narrow(iota((16, CHUNK), 0) & 7)
+    count_is = narrow(iota((16, WIDE), 0) & 7)
     one = jnp.ones((), BF16)
     zero = jnp.zeros((), BF16)
 
     def tally(spread, row, high, low, owner, chunks, index, counting):
         total = None
         for chunk in chunks:
-            start = chunk * CHUNK
+            start = chunk * WIDE
             left, right, mark = [], [], []
             for pair in range(2):
                 data = spread[
-                    pl.ds(pl.multiple_of(row + 16 * pair, 16), 16), start : start + CHUNK
+                    pl.ds(pl.multiple_of(row + 16 * pair, 16), 16), start : start + WIDE
                 ]
                 lows = []
                 for sub in range(2):
                     at = owner * 4 + pair * 2 + sub
-                    h = jnp.broadcast_to(high[index, pl.ds(at, 1), start : start + CHUNK], (8, CHUNK))
+                    h = jnp.broadcast_to(high[index, pl.ds(at, 1), start : start + WIDE], (8, WIDE))
                     h = jnp.concatenate([h, h], axis=0).astype(BF16)
                     left.append(jnp.where(h == high_is, one, zero))
                     left.append(jnp.where(h == high_is + 16.0, one, zero))
                     lows.append(
-                        jnp.broadcast_to(low[index, pl.ds(at, 1), start : start + CHUNK], (8, CHUNK))
+                        jnp.broadcast_to(low[index, pl.ds(at, 1), start : start + WIDE], (8, WIDE))
                     )
                 l = jnp.concatenate(lows, axis=0).astype(BF16)
                 for value in range(8):
@@ -259,7 +263,7 @@
                     high_own,
                     low_own,
                     owner,
-                    range(ROWS_DEV // CHUNK),
+                    range(ROWS_DEV // WIDE),
                     index,
                     True,
                 )
@@ -345,7 +349,7 @@
                 high_asked,
                 low_asked,
                 spot * 2 + side,
-                range(low_chunk, high_chunk),
+                range(low_chunk * CHUNK // WIDE, high_chunk * CHUNK // WIDE),
                 index,
                 False,
             )
@@ -382,7 +386,7 @@
             src_ref=half.at[turn, z_to],
             dst_ref=landed.at[turn * 4 + 3 - z_step],
             send_sem=part_send,
-            recv_sem=part_recv,
+            recv_sem=part_recv.at[turn // SPLIT],
             device_id=(spot_of(turn) * 2 + core, z_to),
             device_id_type=MESH,
         )
@@ -427,20 +431,19 @@
     for turn in range(16 - LAG, 16):
         pass_on(jnp.int32(turn))
 
-    others = landed.at[pl.ds(0, 63)]
-    pltpu.make_async_copy(others, others, part_recv).wait()
-
-    def add(step, total):
-        return total + landed[step]
-
-    total = lax.fori_loop(0, 63, add, half[15, z])
     pltpu.make_async_copy(count_landed, count_landed, count_recv).wait()
-
-    def add_count(step, total):
-        return total + count_landed[step]
-
-    count = lax.fori_loop(0, 63, add_count, count_half[15, z])
+    count = count_half[15, z]
+    for step in range(63):
+        count = count + count_landed[step]
     count = jnp.maximum(count, 1.0)
+
+    total = half[15, z]
+    for group, (begin, end) in enumerate(((0, 4 * SPLIT), (4 * SPLIT, 63))):
+        others = landed.at[pl.ds(begin, end - begin)]
+        pltpu.make_async_copy(others, others, part_recv.at[group]).wait()
+        for step in range(begin, end):
+            total = total + landed[step]
+
     for at in range(4):
         means[z, at] = total[at] / count[at : at + 1, :]
 
@@ -453,7 +456,20 @@
             device_id=(rows_at, lax.rem(z + z_step, 4)),
             device_id_type=MESH,
         ).start()
+    all_landed = landed.at[pl.ds(0, 63)]
+    pltpu.make_async_copy(all_landed, all_landed, part_send).wait()
+    pltpu.make_async_copy(count_landed, count_landed, count_send).wait()
+    count_swap.wait_send()
+    rest = send.at[pl.ds(1, DEV - 1)]
+    pltpu.make_async_copy(rest, rest, send_sem).wait()
+
+    def end_core(turn, unused):
+        core_copy(turn).wait_send()
+        return unused
+
+    lax.fori_loop(0, 16, end_core, 0)
     three = means.at[pl.ds(0, 3)]
+    pltpu.make_async_copy(three, three, last_send).wait()
     pltpu.make_async_copy(three, three, last_recv).wait()
     for index, out in ((0, out_first), (1, out_second)):
         for sub in range(4):
@@ -464,19 +480,6 @@
                 ],
                 axis=1,
             )
-
-    pltpu.make_async_copy(three, three, last_send).wait()
-    pltpu.make_async_copy(others, others, part_send).wait()
-    pltpu.make_async_copy(count_landed, count_landed, count_send).wait()
-    count_swap.wait_send()
-    rest = send.at[pl.ds(1, DEV - 1)]
-    pltpu.make_async_copy(rest, rest, send_sem).wait()
-
-    def end_core(turn, unused):
-        core_copy(turn).wait_send()
-        return unused
-
-    lax.fori_loop(0, 16, end_core, 0)
 
 
 def hand_on(first, second, out_first, out_second):
@@ -500,6 +503,7 @@
             vmem((ROWS_DEV, D), BF16),
             vmem((CENT_DEV, D), BF16),
             vmem((ROWS_DEV, 128), I32),
+            vmem((ROWS_DEV, ROWS_DEV), BF16),
             vmem((DEV, 9, 128), I32),
             vmem((DEV, 9, 128), I32),
             vmem((D, ROWS_DEV), BF16),
@@ -524,7 +528,7 @@
             dma((16,)),
             dma((16,)),
             dma,
-            dma,
+            dma((2,)),
             dma,
             dma,
             dma,

time: 58.4 us -> 56.7 us (0.971)
  Pallas kernels: 57.5 us -> 55.9 us
    pallas_call x1, Pallas kernels: 56.1 us -> 54.5 us  [on_device(): pl.pallas_call(kernel, out_shape=[jax.ShapeDtypeStruct((32, K), F32)] * 2...]
where the time goes in v5:
time: 56.7 us; the launch traced here: 56.6 us
  Pallas kernels  55.9 us (99%)
  between operations  0.64 us (1%)
    pallas_call x1, Pallas kernels, on_device(): pl.pallas_call(kernel, out_shape=[jax.ShapeDtypeStruct((32, K), F32)] * 2...  54.5 us
    pallas_call x1, Pallas kernels, on_device(): pl.pallas_call(hand_on, out_shape=[jax.ShapeDtypeStruct((32, K), F32)] *...  1.4 us

profile of v5, /device:TPU:0, one launch (start us, length us, event | category | flops | bytes accessed | tf_op | source)
XLA Modules:
  0.0 56.6 jit_solution(3649430968219087366)
XLA Ops:
  0.6 54.5 %codebooks.1 = (f32[32,256]{1,0:T(8,128)}, f32[32,256]{1,0:T(8,128)}) custom-call(s32[512]{0:T(512)} %ids_hbm.1, s32[2048,128]{1,0:T(8,128)} %bitcast.3, s32[512,128]{1,0:T(8,128)} %first_hbm.1, s32[512,128]{1,0:T(8,128)} %second_hbm.1, bf16[512,1024]{1,0:T(8,128)(2,1)} %vectors_hbm.1, bf16[2048,1024]{1,0:T(8,128)(2,1)} %table_hbm.1), custom_call_target="tpu_custom_call" | custom-call | tf_op jit(solution)/shard_map/codebooks/pallas_call | solution.py:493
  55.1 1.4 %hand_on.1 = (f32[32,256]{1,0:T(8,128)}, f32[32,256]{1,0:T(8,128)}) custom-call(f32[32,256]{1,0:T(8,128)} %get-tuple-element.6.first, f32[32,256]{1,0:T(8,128)} %get-tuple-element.7.second), custom_call_target="tpu_custom_call" | custom-call | tf_op jit(solution)/shard_map/hand_on/pallas_call | solution.py:544

commit v6 on v5

--- a/solution.py
+++ b/solution.py
@@ -537,7 +537,7 @@
             dma,
         ],
         compiler_params=pltpu.CompilerParams(
-            collective_id=0, has_side_effects=True, vmem_limit_bytes=60 * 2**20
+            collective_id=0, has_side_effects=True, vmem_limit_bytes=55130 * 1024
         ),
         name="codebooks",
     )(list_ids, place, codes_first, codes_second, vectors, centroids)
@@ -546,6 +546,7 @@
         out_shape=[jax.ShapeDtypeStruct((32, K), F32)] * 2,
         in_specs=[pl.BlockSpec(memory_space=vmem)] * 2,
         out_specs=[pl.BlockSpec(memory_space=vmem)] * 2,
+        compiler_params=pltpu.CompilerParams(vmem_limit_bytes=2**20),
         name="hand_on",
     )(first, second)
     return (first.T, second.T)

time: 56.7 us -> 55.7 us (0.982)
  Pallas kernels: 55.9 us -> 54.2 us
  local copies, waits for them, and re-layouts: 0 us -> 0.67 us
    pallas_call x1, Pallas kernels: 54.5 us -> 53.6 us  [on_device(): pl.pallas_call(kernel, out_shape=[jax.ShapeDtypeStruct((32, K), F32)] * 2...]
    pallas_call x1, Pallas kernels: 1.4 us -> 0.63 us  [on_device(): pl.pallas_call(hand_on, out_shape=[jax.ShapeDtypeStruct((32, K), F32)] *...]
    unnamed x0 -> x2, local copies, waits for them, and re-layouts: none -> 0.67 us
where the time goes in v6:
time: 55.7 us; the launch traced here: 55.5 us
  Pallas kernels  54.2 us (97%)
  local copies, waits for them, and re-layouts  0.67 us (1%)
  between operations  0.65 us (1%)
    pallas_call x1, Pallas kernels, on_device(): pl.pallas_call(kernel, out_shape=[jax.ShapeDtypeStruct((32, K), F32)] * 2...  53.6 us

profile of v6, /device:TPU:0, one launch (start us, length us, event | category | flops | bytes accessed | tf_op | source)
XLA Modules:
  0.0 55.5 jit_solution(10227223351769653681)
XLA Ops:
  0.6 0.0 copy-start
  0.6 0.7 %copy-done = s32[512]{0:T(512)S(1)} copy-done((s32[512]{0:T(512)S(1)}, s32[512]{0:T(512)}, u32[]{:S(2)}) %copy-start) | copy-done | bytes 2072
  1.3 53.6 %codebooks.1 = (f32[32,256]{1,0:T(8,128)S(1)}, f32[32,256]{1,0:T(8,128)S(1)}) custom-call(s32[512]{0:T(512)S(1)} %copy-done, s32[2048,128]{1,0:T(8,128)} %bitcast.3, s32[512,128]{1,0:T(8,128)} %first_hbm.1, s32[512,128]{1,0:T(8,128)} %second_hbm.1, bf16[512,1024]{1,0:T(8,128)(2,1)} %vectors_hbm.1, bf16[2048,1024]{1,0:T(8,128)(2,1)} %table_hbm.1), custom_call_target="tpu_custom_call" | custom-call | tf_op jit(solution)/shard_map/codebooks/pallas_call | solution.py:493
  54.9 0.6 %hand_on.1 = (f32[32,256]{1,0:T(8,128)}, f32[32,256]{1,0:T(8,128)}) custom-call(f32[32,256]{1,0:T(8,128)S(1)} %get-tuple-element.6.first, f32[32,256]{1,0:T(8,128)S(1)} %get-tuple-element.7.second), custom_call_target="tpu_custom_call" | custom-call | tf_op jit(solution)/shard_map/hand_on/pallas_call | solution.py:544
Async XLA Ops:
  0.6 0.7 %copy-start = (s32[512]{0:T(512)S(1)}, s32[512]{0:T(512)}, u32[]{:S(2)}) copy-start(s32[512]{0:T(512)} %ids_hbm.1) | copy-start | bytes 6148

commit v7 on v6

--- a/solution.py
+++ b/solution.py
@@ -117,9 +117,9 @@
         loads[at].start()
 
     def greet(step, unused):
-        other = lax.rem(me + step, DEV)
+        other = (me + step) & (DEV - 1)
         pl.semaphore_signal(
-            barrier, inc=1, device_id=(other // 4, lax.rem(other, 4)), device_id_type=MESH
+            barrier, inc=1, device_id=(other >> 2, other & 3), device_id_type=MESH
         )
         return unused
 
@@ -171,7 +171,7 @@
     pl.semaphore_wait(barrier, DEV - 1)
 
     def push(step, unused):
-        other = lax.rem(me + step, DEV)
+        other = (me + step) & (DEV - 1)
         pltpu.make_async_remote_copy(
             src_ref=send.at[other],
             dst_ref=recv.at[step],
@@ -238,8 +238,8 @@
         return sums, own_lanes([256, 264, 272, 280]) if counting else None
 
     def spot_of(turn):
-        x_to = lax.rem(x + turn // 4 + 1, 4)
-        y_to = lax.rem(y + lax.rem(turn, 4) + 1, 4)
+        x_to = (x + (turn >> 2) + 1) & 3
+        y_to = (y + turn + 1) & 3
         return x_to * 4 + y_to
 
     loads[3].wait()
@@ -288,7 +288,7 @@
     count_swap.start()
 
     def count_copy(turn, z_step):
-        z_to = lax.rem(z + z_step, 4)
+        z_to = (z + z_step) & 3
         return pltpu.make_async_remote_copy(
             src_ref=count_half.at[turn, z_to],
             dst_ref=count_landed.at[turn * 4 + 3 - z_step],
@@ -299,8 +299,8 @@
         )
 
     def send_counts(step, unused):
-        turn = step // 4
-        count_copy(turn, 3 - lax.rem(step, 4)).start()
+        turn = step >> 2
+        count_copy(turn, 3 - (step & 3)).start()
         return unused
 
     loads[4].wait()
@@ -345,7 +345,7 @@
         for index in range(2):
             sums, unused_count = tally(
                 spread_asked,
-                (lax.rem(spot, 4) * 2 + side) * 32,
+                ((spot & 3) * 2 + side) * 32,
                 high_asked,
                 low_asked,
                 spot * 2 + side,
@@ -381,12 +381,12 @@
         )
 
     def part_copy(turn, z_step):
-        z_to = lax.rem(z + z_step, 4)
+        z_to = (z + z_step) & 3
         return pltpu.make_async_remote_copy(
             src_ref=half.at[turn, z_to],
             dst_ref=landed.at[turn * 4 + 3 - z_step],
             send_sem=part_send,
-            recv_sem=part_recv.at[turn // SPLIT],
+            recv_sem=part_recv.at[jnp.where(turn < SPLIT, 0, 1)],
             device_id=(spot_of(turn) * 2 + core, z_to),
             device_id_type=MESH,
         )

time: 55.7 us -> 54.1 us (0.971)
  Pallas kernels: 54.2 us -> 52.7 us
    pallas_call x1, Pallas kernels: 53.6 us -> 52.1 us  [on_device(): pl.pallas_call(kernel, out_shape=[jax.ShapeDtypeStruct((32, K), F32)] * 2...]
where the time goes in v7:
time: 54.1 us; the launch traced here: 54 us
  Pallas kernels  52.7 us (97%)
  local copies, waits for them, and re-layouts  0.67 us (1%)
  between operations  0.65 us (1%)
    pallas_call x1, Pallas kernels, on_device(): pl.pallas_call(kernel, out_shape=[jax.ShapeDtypeStruct((32, K), F32)] * 2...  52.1 us

profile of v7, /device:TPU:0, one launch (start us, length us, event | category | flops | bytes accessed | tf_op | source)
XLA Modules:
  0.0 54.0 jit_solution(3422608461930516884)
XLA Ops:
  0.6 0.0 copy-start
  0.6 0.7 %copy-done = s32[512]{0:T(512)S(1)} copy-done((s32[512]{0:T(512)S(1)}, s32[512]{0:T(512)}, u32[]{:S(2)}) %copy-start) | copy-done | bytes 2072
  1.3 52.1 %codebooks.1 = (f32[32,256]{1,0:T(8,128)S(1)}, f32[32,256]{1,0:T(8,128)S(1)}) custom-call(s32[512]{0:T(512)S(1)} %copy-done, s32[2048,128]{1,0:T(8,128)} %bitcast.3, s32[512,128]{1,0:T(8,128)} %first_hbm.1, s32[512,128]{1,0:T(8,128)} %second_hbm.1, bf16[512,1024]{1,0:T(8,128)(2,1)} %vectors_hbm.1, bf16[2048,1024]{1,0:T(8,128)(2,1)} %table_hbm.1), custom_call_target="tpu_custom_call" | custom-call | tf_op jit(solution)/shard_map/codebooks/pallas_call | solution.py:493
  53.4 0.6 %hand_on.1 = (f32[32,256]{1,0:T(8,128)}, f32[32,256]{1,0:T(8,128)}) custom-call(f32[32,256]{1,0:T(8,128)S(1)} %get-tuple-element.6.first, f32[32,256]{1,0:T(8,128)S(1)} %get-tuple-element.7.second), custom_call_target="tpu_custom_call" | custom-call | tf_op jit(solution)/shard_map/hand_on/pallas_call | solution.py:544
Async XLA Ops:
  0.6 0.7 %copy-start = (s32[512]{0:T(512)S(1)}, s32[512]{0:T(512)}, u32[]{:S(2)}) copy-start(s32[512]{0:T(512)} %ids_hbm.1) | copy-start | bytes 6148
